TPU v7x, 32 devices: a whole 2x2x4 slice. The times are simulated.
32 devices in a mesh: groups: 2 (over x), ctx: 16 (over z, y, core).
Axes of the slice: x: 2, y: 2, z: 4, core: 2. Of those that a mesh axis runs over, the one named last changes fastest.
Arguments:
- residual: bfloat16 [4096, 2048], P(('groups', 'ctx')), parts along dimension 0, may hold values from -200 to 200
- queries: bfloat16 [4096, 2048], P(('groups', 'ctx')), parts along dimension 0, may hold values from -64 to 64
- keys: bfloat16 [4096, 256], P(('groups', 'ctx')), parts along dimension 0, may hold values from -64 to 64
- values: bfloat16 [4096, 256], P(('groups', 'ctx')), parts along dimension 0, may hold values from -6 to 6
- block_order: int32 [32], P('groups'), parts along dimension 0, may hold values from 0 to 3, as said below
- routes: int32 [4096, 8], P(('groups', 'ctx')), parts along dimension 0, may hold values from 0 to 15, as said below
- route_weights: float32 [4096, 8], P(('groups', 'ctx')), parts along dimension 0, may hold values from 0.1 to 1
- out_weight: bfloat16 [2048, 2048], P(None, 'ctx'), may hold values from -0.125 to 0.125
- norm_gain: float32 [2048], replicated, may hold values from 0.5 to 1.5
- w_gate_up: bfloat16 [16, 2048, 1536], P('ctx'), may hold values from -0.125 to 0.125
- w_down: bfloat16 [16, 768, 2048], P('ctx'), may hold values from -0.21875 to 0.21875
Outputs:
- context: bfloat16 [4096, 2048], P(('groups', 'ctx')), parts along dimension 0
- mixed: bfloat16 [4096, 2048], P(('groups', 'ctx')), parts along dimension 0
There are 2 independent parts, one for each index of `groups`. A program takes and returns all parts, laid end to end along the dimension named above; an argument that names none is the same for every part. Nothing has to cross between parts.
Inputs may be any that keep to these rules, and one draw needn't show every extreme that they name: `block_order`: for each i below 4, the entries at the indices congruent to i modulo 4 hold every number from 0 to 3 once. `routes`: each token names 8 different experts. Among the tokens of one device no expert is named more than 72 times, and some expert is named exactly 72 times by the tokens of every device.
All inputs are finite; a program needn't handle non-finite values.
Results may differ from a plain program's by a relative error of at most 0.005.
Values may be sent and summed in bfloat16 or wider, within the bound.
A program may use at most 128 MiB of HBM per device.

v0:
```python
import jax
import jax.numpy as jnp
from jax import lax
from jax.sharding import PartitionSpec as P

D = 2048
HEAD_SIZE = 128
FF = 768
QUERY_HEADS = 16
KEY_VALUE_HEADS = 2
TOPK = 8
SEQS = 4


def shifted(array, axis, by):
    devices = lax.axis_size(axis)
    return lax.ppermute(array, axis, [(i, (i + by) % devices) for i in range(devices)])


def local(
    residual,
    queries,
    keys,
    values,
    block_order,
    routes,
    route_weights,
    out_weight,
    norm_gain,
    w_gate_up,
    w_down,
):
    device_row_count = queries.shape[0]
    query_group_width = QUERY_HEADS // KEY_VALUE_HEADS
    devices = lax.axis_size("ctx")
    cycle_length = devices // SEQS
    own_index = lax.axis_index("ctx")
    full_weight = lax.all_gather(out_weight, "ctx", axis=1, tiled=True)
    query_position = block_order[own_index]
    query_head_rows = (
        queries.reshape(device_row_count, KEY_VALUE_HEADS, query_group_width, HEAD_SIZE)
        .transpose(1, 2, 0, 3)
        .reshape(KEY_VALUE_HEADS, query_group_width * device_row_count, HEAD_SIZE)
    )
    query_offset = jnp.arange(query_group_width * device_row_count) % device_row_count
    key_offset = jnp.arange(device_row_count)
    scale = HEAD_SIZE ** (-0.5)

    def update(carry, key_value_tuple, key_position):
        summed, running_max, totals = carry
        local_key_block = key_value_tuple[0].reshape(device_row_count, KEY_VALUE_HEADS, HEAD_SIZE)
        local_value_block = key_value_tuple[1].reshape(device_row_count, KEY_VALUE_HEADS, HEAD_SIZE)
        scores = (
            jnp.einsum(
                "hqd,khd->hqk", query_head_rows, local_key_block, preferred_element_type=jnp.float32
            )
            * scale
        )
        visible = (
            key_position * device_row_count + key_offset[None, :]
            <= query_position * device_row_count + query_offset[:, None]
        )
        scores = jnp.where(visible[None], scores, -jnp.inf)
        new_max = jnp.maximum(running_max, jnp.max(scores, axis=-1))
        factor = jnp.exp(running_max - new_max)
        weights = jnp.exp(scores - new_max[..., None])
        totals = totals * factor + jnp.sum(weights, axis=-1)
        summed = summed * factor[..., None] + jnp.einsum(
            "hqk,khd->hqd",
            weights.astype(jnp.bfloat16),
            local_value_block,
            preferred_element_type=jnp.float32,
        )
        return (summed, new_max, totals)

    initial = (
        jnp.zeros((KEY_VALUE_HEADS, query_group_width * device_row_count, HEAD_SIZE), jnp.float32),
        jnp.full((KEY_VALUE_HEADS, query_group_width * device_row_count), -jnp.inf, jnp.float32),
        jnp.zeros((KEY_VALUE_HEADS, query_group_width * device_row_count), jnp.float32),
    )
    local_pair = jnp.stack([keys, values])
    carry = update(initial, local_pair, query_position)

    def advance(step, state):
        current, moving = state
        moving = shifted(moving, "ctx", SEQS)
        anchor = jnp.mod(own_index - SEQS * step, devices)
        key_position = block_order[anchor]
        current = lax.cond(
            key_position <= query_position,
            lambda inner: update(inner, moving, key_position),
            lambda inner: inner,
            current,
        )
        return (current, moving)

    carry, passed = lax.fori_loop(1, cycle_length, advance, (carry, local_pair))
    summed, running_max, totals = carry
    context = (
        (summed / totals[..., None])
        .reshape(KEY_VALUE_HEADS, query_group_width, device_row_count, HEAD_SIZE)
        .transpose(2, 0, 1, 3)
        .reshape(device_row_count, QUERY_HEADS * HEAD_SIZE)
        .astype(jnp.bfloat16)
    )
    projected = jnp.dot(context, full_weight, preferred_element_type=jnp.float32)
    updated = residual.astype(jnp.float32) + projected
    normed = (
        updated * lax.rsqrt(jnp.mean(updated * updated, axis=-1, keepdims=True) + 1e-06) * norm_gain
    ).astype(jnp.bfloat16)
    experts = devices * w_gate_up.shape[0]
    capacity = 9 * device_row_count * TOPK // (8 * experts)
    expert_ids = routes.reshape(-1)
    one_hot = (expert_ids[:, None] == jnp.arange(experts, dtype=jnp.int32)[None, :]).astype(
        jnp.int32
    )
    ranks = jnp.sum(jnp.cumsum(one_hot, axis=0) * one_hot, axis=1) - 1
    target = expert_ids * capacity + ranks
    source_row = jnp.arange(device_row_count * TOPK) // TOPK
    outgoing = (
        jnp.zeros((experts * capacity, D), jnp.bfloat16)
        .at[target]
        .set(normed[source_row])
        .reshape(experts, capacity, D)
    )
    arrived = lax.all_to_all(outgoing, "ctx", split_axis=0, concat_axis=0, tiled=True)
    flat = arrived.reshape(-1, D)
    both = jnp.dot(flat, w_gate_up[0], preferred_element_type=jnp.float32)
    hidden = (jax.nn.silu(both[:, :FF]) * both[:, FF:]).astype(jnp.bfloat16)
    result = (
        jnp.dot(hidden, w_down[0], preferred_element_type=jnp.float32)
        .astype(jnp.bfloat16)
        .reshape(arrived.shape)
    )
    returned = lax.all_to_all(result, "ctx", split_axis=0, concat_axis=0, tiled=True)
    gathered = returned.reshape(-1, D)[target].reshape(device_row_count, TOPK, D)
    gates = route_weights / jnp.sum(route_weights, axis=-1, keepdims=True)
    mixed = updated
    for slot in range(TOPK):
        mixed = mixed + gates[:, slot : slot + 1] * gathered[:, slot].astype(jnp.float32)
    return (context, mixed.astype(jnp.bfloat16))


def solution(mesh):
    placed = (
        P(("groups", "ctx"), None),
        P(("groups", "ctx"), None),
        P(("groups", "ctx"), None),
        P(("groups", "ctx"), None),
        P("groups"),
        P(("groups", "ctx"), None),
        P(("groups", "ctx"), None),
        P(None, "ctx"),
        P(),
        P("ctx", None, None),
        P("ctx", None, None),
    )
    return jax.shard_map(
        local,
        mesh=mesh,
        in_specs=placed,
        out_specs=(P(("groups", "ctx"), None), P(("groups", "ctx"), None)),
        check_vma=False,
    )
```

profile of v0, /device:TPU:10, one launch (start us, length us, event | category | flops | bytes accessed | tf_op | source)
XLA Modules:
  0.0 404.0 jit_solution(8898957640358070973)
XLA Ops:
  7.2 0.0 copy-start
  7.2 0.0 copy-start.4
  7.2 0.0 copy-start.9
  7.2 0.0 all-gather.2.cloned.1.call-start
  7.2 0.7 all-gather.2.cloned.1.call-update
  7.9 0.9 copy.32
  8.9 0.1 eq.39
  9.0 0.1 eq.35
  9.1 1.1 copy.58
  10.2 0.9 copy.24
  11.1 0.9 copy.28
  12.1 1.0 copy.29
  13.1 1.3 dynamic_slice.13
  15.1 0.7 pad_maximum_fusion
  15.7 0.0 copy-start.5
  15.8 0.1 broadcast_compare_fusion.1
  15.9 1.4 fusion.49
  17.3 0.2 fusion.29
  17.5 0.0 copy-done.4
  17.5 1.6 convolution_add_fusion.2
  19.1 0.0 copy-done.9
  19.1 0.0 copy-done.5
  19.1 0.0 copy-start.6
  19.1 38.9 %while.22 = (s32[]{:T(128)}, f32[2,1024,128]{2,1,0:T(8,128)}, f32[2,1024]{1,0:T(2,128)S(1)}, f32[2,1024]{1,0:T(2,128)S(1)}, bf16[2,128,256]{1,2,0:T(8,128)(2,1)S...) while((s32[]{:T(128)}, f32[2,1024,128]{2,1,0:T(8,128)}, ...), condition=%wide.region_7.8_spmd.clone, body=%wide.region_2.7_spmd.clone.sunk | while | flops 136719504 | bytes 7379506 | solution.py:97
  19.1 1.6 collective-permute-start
  20.7 0.6 dynamic_slice.16
  22.6 6.4 %collective-permute-done = bf16[2,128,256]{1,2,0:T(8,128)(2,1)S(1)} collective-permute-done((bf16[2,128,256]{1,2,0:T(8,128)(2,1)S(1)}, bf16[2,128,256]{1,2,0:T(8,128)(2,1)S(1)}, u32[]{:S(2)}, u32[]{:S(2)}) %collective-permute-start) | collective-permute-done | bytes 131104 | tf_op jit(solution)/shard_map/while/body/eval_jaxpr/ppermute | solution.py:17
  29.1 8.4 %collective-permute-start = (bf16[2,128,256]{1,2,0:T(8,128)(2,1)S(1)}, bf16[2,128,256]{1,2,0:T(8,128)(2,1)S(1)}, u32[]{:S(2)}, u32[]{:S(2)}) collective-permute-start(bf16[2,128,256]{1,2,0:T(8,128)(2,1)S(1)} %get-tuple-element.515), channel_id=1, source_target_pairs={{0,4},{1,5},{2,6},{3,7},{4,8},{5,9},{6,10},{7,11},{8,12},{9,13},{1... | collective-permute-start | bytes 393224 | tf_op jit(solution)/shard_map/while/body/eval_jaxpr/ppermute | solution.py:17
  37.6 0.6 dynamic_slice.16
  39.5 4.5 %collective-permute-done = bf16[2,128,256]{1,2,0:T(8,128)(2,1)S(1)} collective-permute-done((bf16[2,128,256]{1,2,0:T(8,128)(2,1)S(1)}, bf16[2,128,256]{1,2,0:T(8,128)(2,1)S(1)}, u32[]{:S(2)}, u32[]{:S(2)}) %collective-permute-start) | collective-permute-done | bytes 131104 | tf_op jit(solution)/shard_map/while/body/eval_jaxpr/ppermute | solution.py:17
  44.0 2.5 collective-permute-start
  46.5 0.6 dynamic_slice.16
  48.4 9.5 %collective-permute-done = bf16[2,128,256]{1,2,0:T(8,128)(2,1)S(1)} collective-permute-done((bf16[2,128,256]{1,2,0:T(8,128)(2,1)S(1)}, bf16[2,128,256]{1,2,0:T(8,128)(2,1)S(1)}, u32[]{:S(2)}, u32[]{:S(2)}) %collective-permute-start) | collective-permute-done | bytes 131104 | tf_op jit(solution)/shard_map/while/body/eval_jaxpr/ppermute | solution.py:17
  58.0 1.6 divide_convert_fusion
  59.6 0.3 copy.30
  59.9 0.9 copy.97
  60.9 4.5 %reduce-window.6 = s32[16,8,128]{2,1,0:T(8,128)S(1)} reduce-window(s32[16,8,128]{2,1,0:T(8,128)S(1)} %fusion.39, s32[]{:T(128)} %constant.121.clone.1), window={size=1x1x128 pad=0_0x0_0x127_0}, to_apply=%region_9.10 | reduce-window | flops 2080768 | bytes 131076 | tf_op jit(solution)/shard_map/reduce-window
  65.4 0.1 slice.92
  65.5 0.1 copy.34
  65.6 0.1 copy.35
  65.7 0.0 copy-done.6
  65.7 0.1 copy.31
  65.8 0.1 mul.174
  65.9 0.1 broadcast_add_fusion.1
  66.1 27.9 %all-gather.2.cloned.1.call-done = bf16[2048,2048]{1,0:T(8,128)(2,1)} async-done(((bf16[2048,128]{1,0:T(8,128)(2,1)}), bf16[2048,2048]{1,0:T(8,128)(2,1)}) %all-gather.2.cloned.1.call-update) | async-done | bytes 8388624 | tf_op jit(solution)/shard_map/all_gather | solution.py:38
  94.0 5.0 %multiply_reduce_fusion = (f32[128]{0:T(128)S(1)}, f32[128,2048]{1,0:T(8,128)S(1)}) fusion(bf16[128,2048]{1,0:T(8,128)(2,1)} %bitcast.138, bf16[2048,2048]{1,0:T(8,128)(2,1)} %all-gather.2.cloned.1.call-done, bf16[128,2048]{1,0:T(8,128)(2,1)} %param.15), kind=kOutput, calls=%fused_computation.52 | convolution fusion | flops 1074790272 | bytes 10486272 | tf_op jit(solution)/shard_map/dot_general | solution.py:106
  99.0 0.0 copy-start.2
  99.0 1.0 copy-done.2
  100.0 0.0 copy-done.8
  100.0 0.9 multiply_convert_fusion
  101.0 23.8 %scatter_custom_fusion = bf16[1152,2048]{1,0:T(8,128)(2,1)} fusion(s32[1024]{0:T(1024)S(1)} %bitcast.148, bf16[128,2048]{1,0:T(8,128)(2,1)} %multiply_convert_fusion, s32[1024]{0:T(1024)S(1)} %broadcast_clamp_fusion.1, bf16[]{:T(256)} %constant.129.clone.1), kind=kCustom, calls=%fused_computation.23 | custom fusion | bytes 4719104 | tf_op jit(solution)/shard_map/scatter | solution.py:123
  124.7 110.4 %all_to_all.10 = bf16[16,72,2048]{2,1,0:T(8,128)(2,1)S(1)} all-to-all(bf16[16,72,2048]{2,1,0:T(8,128)(2,1)} %bitcast.133), channel_id=1, replica_groups=mesh['groups'=2,'ctx'=16] {'ctx'}, dimensions={0} | all-to-all | bytes 9437184 | tf_op jit(solution)/shard_map/all_to_all | solution.py:126
  235.2 9.7 %fusion.10 = f32[1152,1536]{1,0:T(8,128)S(1)} fusion(bf16[1152,2048]{1,0:T(8,128)(2,1)S(1)} %bitcast.137, bf16[1,2048,1536]{2,1,0:T(8,128)(2,1)} %param.24), kind=kOutput, calls=%fused_computation.21 | convolution fusion | flops 7247757312 | bytes 18087936 | tf_op jit(solution)/shard_map/dot_general | solution.py:128
  244.8 0.0 copy-done
  244.9 5.6 %convolution_convert_fusion = bf16[1152,2048]{1,0:T(8,128)(2,1)} fusion(bf16[1,768,2048]{2,1,0:T(8,128)(2,1)S(1)} %copy-done, f32[1152,1536]{1,0:T(8,128)S(1)} %fusion.10), kind=kOutput, calls=%fused_computation.20 | convolution fusion | flops 3631546368 | bytes 14942208 | tf_op jit(solution)/shard_map/dot_general | solution.py:131
  250.5 5.0 %all-to-all-start.1 = ((bf16[16,72,2048]{2,1,0:T(8,128)(2,1)}), bf16[16,72,2048]{2,1,0:T(8,128)(2,1)}, u32[]{:S(2)}, u32[]{:S(2)}) async-start(bf16[16,72,2048]{2,1,0:T(8,128)(2,1)} %bitcast.136), calls=%async_computation.1 | async-start | bytes 9437184 | tf_op jit(solution)/shard_map/all_to_all | solution.py:135
  255.5 0.0 copy-done.7
  255.6 102.0 %all-to-all-done.1 = bf16[16,72,2048]{2,1,0:T(8,128)(2,1)} async-done(((bf16[16,72,2048]{2,1,0:T(8,128)(2,1)}), bf16[16,72,2048]{2,1,0:T(8,128)(2,1)}, u32[]{:S(2)}, u32[]{:S(2)}) %all-to-all-start.1) | async-done | bytes 4718624 | tf_op jit(solution)/shard_map/all_to_all | solution.py:135
  357.5 11.8 %gather_fusion = bf16[1024,2048]{1,0:T(8,128)(2,1)} fusion(bf16[1152,2048]{1,0:T(8,128)(2,1)} %bitcast.20, s32[1024]{0:T(1024)S(1)} %broadcast_clamp_fusion), kind=kCustom, calls=%fused_computation.1 | custom fusion | bytes 8392704 | tf_op jit(solution)/shard_map/gather | solution.py:136
  369.4 22.3 %fusion.48 = (bf16[128,1,2048]{2,1,0:T(2,128)(2,1)S(1)}, bf16[128,1,2048]{2,1,0:T(2,128)(2,1)S(1)}, bf16[128,1,2048]{2,1,0:T(2,128)(2,1)S(1)}, bf16[128,1,2048]{...) fusion(bf16[128,8,2048]{2,1,0:T(8,128)(2,1)} %bitcast.130), kind=kLoop, calls=%fused_computation.112 | loop fusion | bytes 8388608 | tf_op jit(solution)/shard_map/slice | solution.py:140
  391.6 0.0 copy-start.1
  391.7 0.0 copy-done.3
  391.7 5.5 %fusion.21 = bf16[128,2048]{1,0:T(8,128)(2,1)} fusion(f32[128,2048]{1,0:T(8,128)S(1)} %copy-done.3, bf16[128,1,2048]{2,1,0:T(2,128)(2,1)S(1)} %get-tuple-element.415, bf16[128,1,2048]{2,1,0:T(2,128)(2,1)S(1)} %get-tuple-element.409, bf16[128,1,2048]{2,1,0:T(2,128)(2,1)S(1)} %get-tuple-element.410, bf16[128,1,2048]{2,1,0:T(2,128)(2,1)S(1)} %get-tuple-element.411, ...), kind=kLoop, calls=%fused_computation.36 | loop fusion | flops 6553600 | bytes 5771264 | tf_op jit(solution)/shard_map/convert_element_type | solution.py:141
  397.2 0.0 copy-done.1
  (35 shorter events, 0.2 us)
Async XLA Ops:
  7.2 237.7 %copy-start = (bf16[1,768,2048]{2,1,0:T(8,128)(2,1)S(1)}, bf16[1,768,2048]{2,1,0:T(8,128)(2,1)}, u32[]{:S(2)}) copy-start(bf16[1,768,2048]{2,1,0:T(8,128)(2,1)} %param.25) | copy-start | bytes 9437188
  7.2 10.3 %copy-start.4 = (bf16[128,256]{1,0:T(8,128)(2,1)S(1)}, bf16[128,256]{1,0:T(8,128)(2,1)}, u32[]{:S(2)}) copy-start(bf16[128,256]{1,0:T(8,128)(2,1)} %param.18) | copy-start | bytes 196612
  7.2 11.9 %copy-start.9 = (s32[16]{0:T(128)S(1)}, s32[16]{0:T(128)}, u32[]{:S(2)}) copy-start(s32[16]{0:T(128)} %param.19) | copy-start | bytes 196
  7.2 86.8 %all-gather.2.cloned.1.call-start = ((), (), s32[]{:S(2)}) async-start(), calls=%async_computation.2 | async-start | bytes 8912896 | tf_op jit(solution)/shard_map/all_gather | solution.py:38
  15.7 3.3 copy-start.5
  19.1 46.6 %copy-start.6 = (s32[128,8]{0,1:T(8,128)S(1)}, s32[128,8]{0,1:T(8,128)}, u32[]{:S(2)}) copy-start(s32[128,8]{0,1:T(8,128)} %param.20) | copy-start | bytes 12292
  19.1 10.0 %collective-permute-start = (bf16[2,128,256]{1,2,0:T(8,128)(2,1)S(1)}, bf16[2,128,256]{1,2,0:T(8,128)(2,1)S(1)}, u32[]{:S(2)}, u32[]{:S(2)}) collective-permute-start(bf16[2,128,256]{1,2,0:T(8,128)(2,1)S(1)} %get-tuple-element.515), channel_id=1, source_target_pairs={{0,4},{1,5},{2,6},{3,7},{4,8},{5,9},{6,10},{7,11},{8,12},{9,13},{1... | collective-permute-start | bytes 393224 | tf_op jit(solution)/shard_map/while/body/eval_jaxpr/ppermute | solution.py:17
  29.1 14.8 %collective-permute-start = (bf16[2,128,256]{1,2,0:T(8,128)(2,1)S(1)}, bf16[2,128,256]{1,2,0:T(8,128)(2,1)S(1)}, u32[]{:S(2)}, u32[]{:S(2)}) collective-permute-start(bf16[2,128,256]{1,2,0:T(8,128)(2,1)S(1)} %get-tuple-element.515), channel_id=1, source_target_pairs={{0,4},{1,5},{2,6},{3,7},{4,8},{5,9},{6,10},{7,11},{8,12},{9,13},{1... | collective-permute-start | bytes 393224 | tf_op jit(solution)/shard_map/while/body/eval_jaxpr/ppermute | solution.py:17
  44.0 14.0 %collective-permute-start = (bf16[2,128,256]{1,2,0:T(8,128)(2,1)S(1)}, bf16[2,128,256]{1,2,0:T(8,128)(2,1)S(1)}, u32[]{:S(2)}, u32[]{:S(2)}) collective-permute-start(bf16[2,128,256]{1,2,0:T(8,128)(2,1)S(1)} %get-tuple-element.515), channel_id=1, source_target_pairs={{0,4},{1,5},{2,6},{3,7},{4,8},{5,9},{6,10},{7,11},{8,12},{9,13},{1... | collective-permute-start | bytes 393224 | tf_op jit(solution)/shard_map/while/body/eval_jaxpr/ppermute | solution.py:17
  94.0 6.0 %copy-start.8 = (f32[2048]{0:T(1024)S(1)}, f32[2048]{0:T(1024)}, u32[]{:S(2)}) copy-start(f32[2048]{0:T(1024)} %param.23) | copy-start | bytes 24580
  99.0 1.0 copy-start.2
  250.5 5.0 %copy-start.7 = (f32[128,8]{0,1:T(8,128)S(1)}, f32[128,8]{0,1:T(8,128)}, u32[]{:S(2)}) copy-start(f32[128,8]{0,1:T(8,128)} %param.21) | copy-start | bytes 12292
  250.5 107.0 %all-to-all-start.1 = ((bf16[16,72,2048]{2,1,0:T(8,128)(2,1)}), bf16[16,72,2048]{2,1,0:T(8,128)(2,1)}, u32[]{:S(2)}, u32[]{:S(2)}) async-start(bf16[16,72,2048]{2,1,0:T(8,128)(2,1)} %bitcast.136), calls=%async_computation.1 | async-start | bytes 9437184 | tf_op jit(solution)/shard_map/all_to_all | solution.py:135
  369.4 22.3 %copy-start.3 = (f32[128,2048]{1,0:T(8,128)S(1)}, f32[128,2048]{1,0:T(8,128)}, u32[]{:S(2)}) copy-start(f32[128,2048]{1,0:T(8,128)} %copy-done.2) | copy-start | bytes 3145732
  391.6 5.5 %copy-start.1 = (bf16[1,768,2048]{2,1,0:T(8,128)(2,1)S(1)}, bf16[1,768,2048]{2,1,0:T(8,128)(2,1)}, u32[]{:S(2)}) copy-start(bf16[1,768,2048]{2,1,0:T(8,128)(2,1)} %param.25) | copy-start | bytes 9437188
Sparse Core Ops, SparseCore 0:
  10.2 83.8 all-gather.1
where the time goes:
time: 407 us; the launch traced here: 404 us
  waiting for transfers between devices  151 us (37%)
  blocking collectives  110 us (27%)
  local copies, waits for them, and re-layouts  68.8 us (17%)
  matrix products  23.3 us (6%)
  starting transfers between devices  17.6 us (4%)
  between operations  15 us (4%)
  other arithmetic  13.8 us (3%)
    all_to_all x1, blocking collectives, local(): lax.all_to_all(outgoing, 'ctx', split_axis=0, concat_axis=0, tiled=True)  110 us
    all_to_all x1, waiting for transfers between devices, local(): lax.all_to_all(result, 'ctx', split_axis=0, concat_axis=0, tiled=True)  102 us
    all_gather x1, waiting for transfers between devices, local(): full_weight = lax.all_gather(out_weight, 'ctx', axis=1, tiled=True)  27.9 us
    scatter x1, local copies, waits for them, and re-layouts, local(): outgoing = jnp.zeros((experts * capacity, D), jnp.bfloat16).at[target].se...  23.8 us
    slice x1, local copies, waits for them, and re-layouts, local(): gathered[:, slot].astype(jnp.float32)  22.3 us
    ppermute x3, waiting for transfers between devices, shifted(): lax.ppermute(array, axis, [(i, (i + by) % devices) for i in range(devices)])  20.4 us
    ppermute x3, starting transfers between devices, shifted(): lax.ppermute(array, axis, [(i, (i + by) % devices) for i in range(devices)])  12.6 us
    gather x1, local copies, waits for them, and re-layouts, local(): returned.reshape(-1, D)[target].reshape(device_row_count, TOPK, D)  11.8 us
  transfers between devices with their start and end apart: 5, of which 5 were waited for; matrix products, arithmetic and copies ran while one was open for 5% of the time, Pallas kernels for 0%

commit v1 on v0

--- a/solution.py
+++ b/solution.py
@@ -1,6 +1,10 @@
+import functools
+
 import jax
 import jax.numpy as jnp
 from jax import lax
+from jax.experimental import pallas as pl
+from jax.experimental.pallas import tpu as pltpu
 from jax.sharding import PartitionSpec as P
 
 D = 2048
@@ -15,6 +19,357 @@
 def shifted(array, axis, by):
     devices = lax.axis_size(axis)
     return lax.ppermute(array, axis, [(i, (i + by) % devices) for i in range(devices)])
+
+
+VMEM_BYTES = 60 * 2**20
+
+
+def put(src, dst, send_sem, recv_sem, to):
+    return pltpu.make_async_remote_copy(
+        src_ref=src,
+        dst_ref=dst,
+        send_sem=send_sem,
+        recv_sem=recv_sem,
+        device_id={"ctx": to},
+        device_id_type=pl.DeviceIdType.MESH,
+    )
+
+
+def plane_at(step, z, planes):
+    short = jnp.minimum(z, planes - 1 - z)
+    sign = jnp.where(2 * z < planes - 1, 1, -1)
+    near = (step + 1) // 2 * (2 * (step % 2) - 1)
+    return z + sign * jnp.where(step <= 2 * short, near, step - short)
+
+
+def expert_kernel(
+    planes,
+    cap,
+    normed_ref,
+    updated_ref,
+    gates_ref,
+    up_hbm,
+    down_hbm,
+    out_ref,
+    rows_all,
+    contrib,
+    from_core,
+    from_y,
+    from_z,
+    w_up,
+    w_down,
+    ranks,
+    picked,
+    act,
+    w_sem,
+    recv,
+    up_s,
+    dn_s,
+    y_s,
+    c_s,
+    rc_s,
+    rc_r,
+    ry_s,
+    ry_r,
+    rz_s,
+    rz_r,
+):
+    n, width = normed_ref.shape
+    hidden = w_down.shape[0]
+    pair = 2 * n
+    me = lax.axis_index("ctx")
+    z, place = me // SEQS, me % SEQS
+    y, c = place // 2, place % 2
+    at_y = z * SEQS + (1 - y) * 2 + c
+    at_core = z * SEQS + y * 2 + (1 - c)
+    above, below = z < planes - 1, z > 0
+
+    def block(ref, index):
+        return ref.at[pl.ds(pl.multiple_of(index * n, n), n)]
+
+    load_up = pltpu.make_async_copy(up_hbm.at[0], w_up, w_sem.at[0])
+    load_down = pltpu.make_async_copy(down_hbm.at[0], w_down, w_sem.at[1])
+    load_up.start()
+    load_down.start()
+
+    barrier = pltpu.get_barrier_semaphore()
+
+    def greet(to):
+        pl.semaphore_signal(
+            barrier, inc=1, device_id={"ctx": to}, device_id_type=pl.DeviceIdType.MESH
+        )
+
+    greet(at_y)
+    greet(at_core)
+    pl.when(above)(lambda: greet(me + SEQS))
+    pl.when(below)(lambda: greet(me - SEQS))
+    block(rows_all, me)[...] = normed_ref[...]
+    pl.semaphore_wait(barrier, 2 + jnp.where(above, 1, 0) + jnp.where(below, 1, 0))
+
+    def gather_copy(index, sem, to):
+        return put(block(rows_all, index), block(rows_all, index), sem, recv.at[index], to)
+
+    def forwards(p):
+        index = p * SEQS + place
+        return (
+            (above & (p <= z), gather_copy(index, up_s.at[p], me + SEQS)),
+            (below & (p >= z), gather_copy(index, dn_s.at[p], me - SEQS)),
+            (None, gather_copy(index, y_s.at[p], at_y)),
+            (None, gather_copy(index, c_s.at[p * 2 + y], at_core)),
+        )
+
+    def second_forward(p):
+        return gather_copy(p * SEQS + (1 - y) * 2 + c, c_s.at[p * 2 + 1 - y], at_core)
+
+    def core_return(p, row):
+        return put(
+            block(contrib, p * SEQS + row * 2 + 1 - c),
+            block(from_core, p * 2 + row),
+            rc_s.at[p * 2 + row],
+            rc_r.at[p * 2 + row],
+            at_core,
+        )
+
+    def y_return(p):
+        return put(
+            block(contrib, p * SEQS + (1 - y) * 2 + c),
+            block(from_y, p),
+            ry_s.at[p],
+            ry_r.at[p],
+            at_y,
+        )
+
+    def z_return(p, slot, to):
+        return put(
+            block(contrib, p * SEQS + place), block(from_z, slot), rz_s.at[p], rz_r.at[slot], to
+        )
+
+    shape = (pair, pair)
+    earlier = lax.broadcasted_iota(jnp.int32, shape, 0)
+    later = lax.broadcasted_iota(jnp.int32, shape, 1)
+    before = (earlier < later) & (earlier // n == later // n)
+    routed = gates_ref[...] > 0
+    count = jnp.dot(
+        routed.astype(jnp.bfloat16), before.astype(jnp.bfloat16), preferred_element_type=jnp.float32
+    ).astype(jnp.int32)
+    offset = lax.broadcasted_iota(jnp.int32, count.shape, 1) // n * cap
+    ranks[...] = jnp.where(routed, count + offset, -1)
+
+    def compute(p):
+        parts = []
+        for half in range(2):
+            row = pl.ds(p * 2 + half, 1)
+            hit = lax.broadcasted_iota(jnp.int32, (2 * cap, pair), 0) == ranks[row, :]
+            gate = jnp.sum(jnp.where(hit, gates_ref[row, :], 0.0), axis=1, keepdims=True)
+            choose = hit.astype(jnp.float32).astype(jnp.bfloat16)
+            parts.append((choose, gate))
+        tile = 512
+
+        def pick(j, carry):
+            cols = pl.ds(pl.multiple_of(j * tile, tile), tile)
+            for half in range(2):
+                source = pl.ds(pl.multiple_of((p * 2 + half) * pair, pair), pair)
+                picked[pl.ds(half * 2 * cap, 2 * cap), cols] = jnp.dot(
+                    parts[half][0], rows_all[source, cols], preferred_element_type=jnp.float32
+                ).astype(jnp.bfloat16)
+            return carry
+
+        lax.fori_loop(0, width // tile, pick, 0)
+        narrow = 256
+
+        def gate_up(j, carry):
+            first = pl.ds(pl.multiple_of(j * narrow, narrow), narrow)
+            second = pl.ds(pl.multiple_of(hidden + j * narrow, narrow), narrow)
+            v = jnp.dot(picked[...], w_up[:, first], preferred_element_type=jnp.float32)
+            u = jnp.dot(picked[...], w_up[:, second], preferred_element_type=jnp.float32)
+            act[:, first] = (v / (1.0 + jnp.exp(-v)) * u).astype(jnp.bfloat16)
+            return carry
+
+        lax.fori_loop(0, hidden // narrow, gate_up, 0)
+
+        def down(j, carry):
+            cols = pl.ds(pl.multiple_of(j * tile, tile), tile)
+            for half in range(2):
+                choose, gate = parts[half]
+                source = pl.ds(pl.multiple_of((p * 2 + half) * pair, pair), pair)
+                result = jnp.dot(
+                    act[pl.ds(half * 2 * cap, 2 * cap), :],
+                    w_down[:, cols],
+                    preferred_element_type=jnp.float32,
+                )
+                contrib[source, cols] = lax.dot_general(
+                    choose,
+                    (result * gate).astype(jnp.bfloat16),
+                    (((0,), (0,)), ((), ())),
+                    preferred_element_type=jnp.float32,
+                ).astype(jnp.bfloat16)
+            return carry
+
+        lax.fori_loop(0, width // tile, down, 0)
+
+    def advance(k, carry):
+        @pl.when(k < planes)
+        def _():
+            p = plane_at(k, z, planes)
+
+            @pl.when(k > 0)
+            def _():
+                gather_copy(p * SEQS + place, y_s.at[p], at_y).wait_recv()
+
+            for condition, copy in forwards(p):
+                if condition is None:
+                    copy.start()
+                else:
+                    pl.when(condition)(copy.start)
+
+        @pl.when(k > 0)
+        def _():
+            p = plane_at(k - 1, z, planes)
+            second_forward(p).wait_recv()
+            second_forward(p).start()
+            for row in range(2):
+                gather_copy(p * SEQS + row * 2 + 1 - c, c_s.at[0], at_core).wait_recv()
+
+            @pl.when(k == 1)
+            def _():
+                load_up.wait()
+                load_down.wait()
+
+            compute(p)
+            for row in range(2):
+                core_return(p, row).start()
+
+        return carry
+
+    lax.fori_loop(0, planes + 1, advance, 0)
+    chunk = 16
+
+    def add_up(target, terms):
+        def some(i, carry):
+            here = pl.ds(pl.multiple_of(i * chunk, chunk), chunk)
+            total = terms[0][here, :].astype(jnp.float32)
+            for term in terms[1:]:
+                total = total + term[here, :].astype(jnp.float32)
+            target[here, :] = total.astype(target.dtype)
+            return carry
+
+        lax.fori_loop(0, n // chunk, some, 0)
+
+    def core_sum(i, carry):
+        p = plane_at(planes - 1 - i, z, planes)
+        for row in range(2):
+            core_return(p, row).wait_recv()
+        other = block(contrib, p * SEQS + (1 - y) * 2 + c)
+        add_up(other, [other, block(from_core, p * 2 + 1 - y)])
+        y_return(p).start()
+        return carry
+
+    lax.fori_loop(0, planes, core_sum, 0)
+
+    def chain(i, carry):
+        p = plane_at(planes - 1 - i, z, planes)
+        y_return(p).wait_recv()
+        own = block(contrib, p * SEQS + place)
+        add_up(own, [own, block(from_core, p * 2 + y), block(from_y, p)])
+
+        @pl.when(((p < z) & above) | ((p > z) & below))
+        def _():
+            z_return(p, p, at_y).wait_recv()
+            add_up(own, [own, block(from_z, p)])
+
+        @pl.when(p < z)
+        def _():
+            z_return(p, jnp.where(p == z - 1, planes, p), me - SEQS).start()
+
+        @pl.when(p > z)
+        def _():
+            z_return(p, p, me + SEQS).start()
+
+        return carry
+
+    lax.fori_loop(0, planes - 1, chain, 0)
+    y_return(z).wait_recv()
+    mine = block(contrib, me)
+    terms = [updated_ref, mine, block(from_core, z * 2 + y), block(from_y, z)]
+    low, high = block(from_z, z), block(from_z, planes)
+    pl.when(below)(lambda: z_return(z, z, at_y).wait_recv())
+    pl.when(above)(lambda: z_return(z, planes, at_y).wait_recv())
+    pl.when(below & above)(lambda: add_up(out_ref, terms + [low, high]))
+    pl.when(below & jnp.logical_not(above))(lambda: add_up(out_ref, terms + [low]))
+    pl.when(jnp.logical_not(below) & above)(lambda: add_up(out_ref, terms + [high]))
+
+    def finish(p, carry):
+        for condition, copy in forwards(p):
+            if condition is None:
+                copy.wait_send()
+            else:
+                pl.when(condition)(copy.wait_send)
+        second_forward(p).wait_send()
+        for row in range(2):
+            core_return(p, row).wait_send()
+        y_return(p).wait_send()
+        pl.when(p != z)(lambda: z_return(p, p, at_y).wait_send())
+        return carry
+
+    lax.fori_loop(0, planes, finish, 0)
+
+
+def expert_call(normed, updated, gates_here, w_gate_up, w_down, cap):
+    n, width = normed.shape
+    hidden = w_down.shape[1]
+    devices = lax.axis_size("ctx")
+    planes = devices // SEQS
+    vmem = pl.BlockSpec(memory_space=pltpu.VMEM)
+    anywhere = pl.BlockSpec(memory_space=pl.ANY)
+    bf16 = jnp.bfloat16
+    return pl.pallas_call(
+        functools.partial(expert_kernel, planes, cap),
+        out_shape=jax.ShapeDtypeStruct((n, width), bf16),
+        in_specs=[vmem, vmem, vmem, anywhere, anywhere],
+        out_specs=vmem,
+        scratch_shapes=[
+            pltpu.VMEM((devices * n, width), bf16),
+            pltpu.VMEM((devices * n, width), bf16),
+            pltpu.VMEM((2 * planes * n, width), bf16),
+            pltpu.VMEM((planes * n, width), bf16),
+            pltpu.VMEM(((planes + 1) * n, width), bf16),
+            pltpu.VMEM(w_gate_up.shape[1:], bf16),
+            pltpu.VMEM(w_down.shape[1:], bf16),
+            pltpu.VMEM((2 * planes, 2 * n), jnp.int32),
+            pltpu.VMEM((SEQS * cap, width), bf16),
+            pltpu.VMEM((SEQS * cap, hidden), bf16),
+            pltpu.SemaphoreType.DMA((2,)),
+            pltpu.SemaphoreType.DMA((devices,)),
+            pltpu.SemaphoreType.DMA((planes,)),
+            pltpu.SemaphoreType.DMA((planes,)),
+            pltpu.SemaphoreType.DMA((planes,)),
+            pltpu.SemaphoreType.DMA((2 * planes,)),
+            pltpu.SemaphoreType.DMA((2 * planes,)),
+            pltpu.SemaphoreType.DMA((2 * planes,)),
+            pltpu.SemaphoreType.DMA((planes,)),
+            pltpu.SemaphoreType.DMA((planes,)),
+            pltpu.SemaphoreType.DMA((planes,)),
+            pltpu.SemaphoreType.DMA((planes + 1,)),
+        ],
+        compiler_params=pltpu.CompilerParams(
+            collective_id=0, has_side_effects=True, vmem_limit_bytes=VMEM_BYTES
+        ),
+        name="experts",
+    )(normed, updated, gates_here, w_gate_up, w_down)
+
+
+def gates_for_own(routes, route_weights, devices):
+    gates = route_weights / jnp.sum(route_weights, axis=-1, keepdims=True)
+    chosen = routes.T[None] == jnp.arange(devices, dtype=jnp.int32)[:, None, None]
+    table = jnp.sum(jnp.where(chosen, gates.T[None], 0.0), axis=1)
+    everyone = lax.all_gather(table, "ctx", axis=0)
+    mine = lax.dynamic_index_in_dim(everyone, lax.axis_index("ctx"), axis=1, keepdims=False)
+    return mine.reshape(devices // 2, 2 * routes.shape[0])
+
+
+def fits(devices, rows, width, hidden):
+    blocks = 3 * devices + 4
+    return 2 * (blocks * rows * width + 3 * width * hidden) < VMEM_BYTES * 4 // 5
 
 
 def local(
@@ -36,6 +391,7 @@
     cycle_length = devices // SEQS
     own_index = lax.axis_index("ctx")
     full_weight = lax.all_gather(out_weight, "ctx", axis=1, tiled=True)
+    gates_here = gates_for_own(routes, route_weights, devices)
     query_position = block_order[own_index]
     query_head_rows = (
         queries.reshape(device_row_count, KEY_VALUE_HEADS, query_group_width, HEAD_SIZE)
@@ -110,6 +466,9 @@
     ).astype(jnp.bfloat16)
     experts = devices * w_gate_up.shape[0]
     capacity = 9 * device_row_count * TOPK // (8 * experts)
+    if fits(devices, device_row_count, D, FF):
+        mixed = expert_call(normed, updated, gates_here, w_gate_up, w_down, capacity)
+        return (context, mixed)
     expert_ids = routes.reshape(-1)
     one_hot = (expert_ids[:, None] == jnp.arange(experts, dtype=jnp.int32)[None, :]).astype(
         jnp.int32

time: 407 us -> 235 us (0.58)
  Pallas kernels: 0 us -> 125 us
  waiting for transfers between devices: 151 us -> 36.6 us
  blocking collectives: 110 us -> 20.2 us
  local copies, waits for them, and re-layouts: 68.8 us -> 11.3 us
  matrix products: 23.3 us -> 9.52 us
  starting transfers between devices: 17.6 us -> 6.15 us
  other arithmetic: 13.8 us -> 2.59 us
    pallas_call x0 -> x1, Pallas kernels: none -> 125 us  [expert_call(): pl.pallas_call(functools.partial(expert_kernel, planes, cap), out_shape=j...]
    all_to_all x1 -> x0, blocking collectives: 110 us -> none  [local(): lax.all_to_all(outgoing, 'ctx', split_axis=0, concat_axis=0, tiled=True)]
    all_to_all x1 -> x0, waiting for transfers between devices: 102 us -> none  [local(): lax.all_to_all(result, 'ctx', split_axis=0, concat_axis=0, tiled=True)]
    scatter x1 -> x0, local copies, waits for them, and re-layouts: 23.8 us -> none  [local(): outgoing = jnp.zeros((experts * capacity, D), jnp.bfloat16).at[target].se...]
    slice x3 -> x2, local copies, waits for them, and re-layouts: 22.5 us -> 0.02 us  [update(): key_value_tuple[0].reshape(device_row_count, KEY_VALUE_HEADS, HEAD_SIZE)]
    all_gather x0 -> x1, blocking collectives: none -> 20.2 us  [gates_for_own(): everyone = lax.all_gather(table, 'ctx', axis=0)]
    dot_general x2 -> x0, matrix products: 15.3 us -> none  [the longest x1 9.66 us: local(): both = jnp.dot(flat, w_gate_up[0], preferred_element_type=jnp.float32)]
    ppermute x3, waiting for transfers between devices: 20.4 us -> 8.59 us  [shifted(): lax.ppermute(array, axis, [(i, (i + by) % devices) for i in range(devices)])]
  transfers between devices with their start and end apart: 5 -> 4, of which waited for: 5 -> 4; matrix products, arithmetic and copies ran while one was open for 5% -> 7% of each run, Pallas kernels for 0% -> 0%
where the time goes in v1:
time: 235 us; the launch traced here: 233 us
  Pallas kernels  125 us (53%)
  waiting for transfers between devices  36.6 us (16%)
  blocking collectives  20.2 us (9%)
  between operations  14.8 us (6%)
  local copies, waits for them, and re-layouts  11.3 us (5%)
  matrix products  9.52 us (4%)
  loops' own time  6.23 us (3%)
  starting transfers between devices  6.15 us (3%)
  other arithmetic  2.59 us (1%)
    pallas_call x1, Pallas kernels, expert_call(): pl.pallas_call(functools.partial(expert_kernel, planes, cap), out_shape=j...  125 us
    all_gather x1, waiting for transfers between devices, local(): full_weight = lax.all_gather(out_weight, 'ctx', axis=1, tiled=True)  27.4 us
    all_gather x1, blocking collectives, gates_for_own(): everyone = lax.all_gather(table, 'ctx', axis=0)  20.2 us
    ppermute x3, waiting for transfers between devices, shifted(): lax.ppermute(array, axis, [(i, (i + by) % devices) for i in range(devices)])  8.59 us
    ppermute x3, starting transfers between devices, shifted(): lax.ppermute(array, axis, [(i, (i + by) % devices) for i in range(devices)])  6.11 us
    unnamed x17, local copies, waits for them, and re-layouts  5.12 us
    dot_general x1, matrix products, local(): jnp.dot(context, full_weight, preferred_element_type=jnp.float32)  4.81 us
  transfers between devices with their start and end apart: 4, of which 4 were waited for; matrix products, arithmetic and copies ran while one was open for 7% of the time, Pallas kernels for 0%

profile of v1, /device:TPU:10, one launch (start us, length us, event | category | flops | bytes accessed | tf_op | source)
XLA Modules:
  0.0 232.6 jit_solution(12162790854582141597)
XLA Ops:
  7.2 0.0 all-gather.3.cloned.1.call-start
  7.2 0.7 all-gather.3.cloned.1.call-update
  7.9 1.1 copy.45
  9.1 0.1 copy.32
  9.2 1.0 copy.36
  10.2 1.0 copy.37
  11.1 1.2 dynamic_slice.17
  13.0 0.1 broadcast_compare_fusion.1
  13.1 1.2 fusion.26
  14.3 0.2 fusion.11
  14.5 1.3 convolution_add_fusion.2
  15.9 0.0 copy-start.3
  15.9 0.0 copy-start.5
  15.9 0.0 copy-start.2
  15.9 27.6 %while.22 = (s32[]{:T(128)}, f32[2,1024,128]{2,1,0:T(8,128)S(1)}, f32[2,1024]{1,0:T(2,128)S(1)}, f32[2,1024]{1,0:T(2,128)S(1)}, bf16[2,128,256]{1,2,0:T(8,128)(2...) while((s32[]{:T(128)}, f32[2,1024,128]{2,1,0:T(8,128)S(1)}, ...), condition=%wide.region_7.8_spmd.clone, body=%wide.region_2.7_spmd.clone.sunk | while | flops 136719504 | bytes 7379506 | solution.py:453
  15.9 1.6 collective-permute-start
  17.5 1.2 dynamic_slice.22
  20.0 1.2 collective-permute-done
  21.2 2.7 %conditional.3 = ((f32[2,1024,128]{2,1,0:T(8,128)S(1)}, f32[2,1024]{1,0:T(2,128)S(1)}, f32[2,1024]{1,0:T(2,128)S(1)})) conditional(s32[]{:T(128)} %convert_element_type.51, (f32[2,1024,128]{2,1,0:T(8,128)S(1)}, f32[2,1024]{1,0:T(2,128)S(1)}, f32[2,1024]{1,0:T(2,128)S(1)}) %tuple.63, (s32[]{:T(128)}, s32[128]{0:T(128)S(1)}, s32[]{:T(128)}, ...), branch_computations={%region_3.3_spmd, %region_4.6_spmd.clone} | conditional | flops 136718464 | bytes 6583872 | solution.py:445
  22.4 0.1 broadcast_compare_fusion
  22.6 0.4 fusion.25
  23.0 0.2 fusion.5
  23.2 0.7 convolution_add_fusion
  23.9 1.6 collective-permute-start
  25.6 1.2 dynamic_slice.22
  28.0 4.2 %collective-permute-done = bf16[2,128,256]{1,2,0:T(8,128)(2,1)S(1)} collective-permute-done((bf16[2,128,256]{1,2,0:T(8,128)(2,1)S(1)}, bf16[2,128,256]{1,2,0:T(8,128)(2,1)S(1)}, u32[]{:S(2)}, u32[]{:S(2)}) %collective-permute-start) | collective-permute-done | bytes 131104 | tf_op jit(solution)/shard_map/while/body/eval_jaxpr/ppermute | solution.py:21
  32.2 2.7 %conditional.3 = ((f32[2,1024,128]{2,1,0:T(8,128)S(1)}, f32[2,1024]{1,0:T(2,128)S(1)}, f32[2,1024]{1,0:T(2,128)S(1)})) conditional(s32[]{:T(128)} %convert_element_type.51, (f32[2,1024,128]{2,1,0:T(8,128)S(1)}, f32[2,1024]{1,0:T(2,128)S(1)}, f32[2,1024]{1,0:T(2,128)S(1)}) %tuple.63, (s32[]{:T(128)}, s32[128]{0:T(128)S(1)}, s32[]{:T(128)}, ...), branch_computations={%region_3.3_spmd, %region_4.6_spmd.clone} | conditional | flops 136718464 | bytes 6583872 | solution.py:445
  33.5 0.1 broadcast_compare_fusion
  33.6 0.4 fusion.25
  34.0 0.2 fusion.5
  34.2 0.7 convolution_add_fusion
  35.0 2.9 %collective-permute-start = (bf16[2,128,256]{1,2,0:T(8,128)(2,1)S(1)}, bf16[2,128,256]{1,2,0:T(8,128)(2,1)S(1)}, u32[]{:S(2)}, u32[]{:S(2)}) collective-permute-start(bf16[2,128,256]{1,2,0:T(8,128)(2,1)S(1)} %get-tuple-element.499), channel_id=1, source_target_pairs={{0,4},{1,5},{2,6},{3,7},{4,8},{5,9},{6,10},{7,11},{8,12},{9,13},{1... | collective-permute-start | bytes 393224 | tf_op jit(solution)/shard_map/while/body/eval_jaxpr/ppermute | solution.py:21
  37.8 1.2 dynamic_slice.22
  40.3 3.2 %collective-permute-done = bf16[2,128,256]{1,2,0:T(8,128)(2,1)S(1)} collective-permute-done((bf16[2,128,256]{1,2,0:T(8,128)(2,1)S(1)}, bf16[2,128,256]{1,2,0:T(8,128)(2,1)S(1)}, u32[]{:S(2)}, u32[]{:S(2)}) %collective-permute-start) | collective-permute-done | bytes 131104 | tf_op jit(solution)/shard_map/while/body/eval_jaxpr/ppermute | solution.py:21
  43.5 0.3 divide_convert_fusion
  43.9 0.3 copy.38
  44.2 0.1 copy.58
  44.4 0.0 copy-done.3
  44.4 0.0 copy-start.1
  44.4 0.0 copy-start.4
  44.4 0.0 copy-done.5
  44.5 20.2 %all-gather = f32[256,128]{1,0:T(8,128)S(1)} all-gather(f32[16,128]{1,0:T(8,128)S(1)} %select_reduce_fusion), channel_id=2, replica_groups=mesh['groups'=2,'ctx'=16] {'ctx'}, dimensions={0}, use_global_device_ids=true | all-gather | bytes 139264 | tf_op jit(solution)/shard_map/all_gather | solution.py:365
  64.7 0.6 reshape.112.gates_ref
  65.3 27.4 %all-gather.3.cloned.1.call-done = bf16[2048,2048]{1,0:T(8,128)(2,1)} async-done(((bf16[2048,128]{1,0:T(8,128)(2,1)}), bf16[2048,2048]{1,0:T(8,128)(2,1)}) %all-gather.3.cloned.1.call-update) | async-done | bytes 8388624 | tf_op jit(solution)/shard_map/all_gather | solution.py:393
  92.7 0.0 copy-done.2
  92.7 4.8 %multiply_reduce_fusion = (f32[128]{0:T(128)S(1)}, f32[128,2048]{1,0:T(8,128)S(1)}) fusion(bf16[128,2048]{1,0:T(8,128)(2,1)S(1)} %bitcast.53, bf16[2048,2048]{1,0:T(8,128)(2,1)} %all-gather.3.cloned.1.call-done, bf16[128,2048]{1,0:T(8,128)(2,1)S(1)} %copy-done.2), kind=kOutput, calls=%fused_computation.22 | convolution fusion | flops 1074790272 | bytes 10486272 | tf_op jit(solution)/shard_map/dot_general | solution.py:462
  97.5 0.0 copy-start
  97.5 0.0 copy-done.4
  97.5 1.1 multiply_convert_fusion.normed_ref
  98.6 0.0 copy-done.1
  98.6 0.0 copy-done
  98.6 125.2 %experts.1 = bf16[128,2048]{1,0:T(8,128)(2,1)} custom-call(bf16[128,2048]{1,0:T(8,128)(2,1)} %multiply_convert_fusion.normed_ref, f32[128,2048]{1,0:T(8,128)} %copy-done, f32[8,256]{1,0:T(8,128)} %reshape.112.gates_ref, bf16[1,2048,1536]{2,1,0:T(8,128)(2,1)} %up_hbm.1, bf16[1,768,2048]{2,1,0:T(8,128)(2,1)} %down_hbm.1), custom_call_target="tpu_custom_call" | custom-call | tf_op jit(solution)/shard_map/experts/pallas_call | solution.py:325
  223.9 1.9 copy.81
  (34 shorter events, 0.3 us)
Async XLA Ops:
  7.2 85.5 %all-gather.3.cloned.1.call-start = ((), (), s32[]{:S(2)}) async-start(), calls=%async_computation | async-start | bytes 8912896 | tf_op jit(solution)/shard_map/all_gather | solution.py:393
  15.9 28.5 %copy-start.3 = (f32[128,8]{0,1:T(8,128)S(1)}, f32[128,8]{0,1:T(8,128)}, u32[]{:S(2)}) copy-start(f32[128,8]{0,1:T(8,128)} %param.21) | copy-start | bytes 12292
  15.9 28.6 %copy-start.5 = (s32[128,8]{0,1:T(8,128)S(1)}, s32[128,8]{0,1:T(8,128)}, u32[]{:S(2)}) copy-start(s32[128,8]{0,1:T(8,128)} %param.20) | copy-start | bytes 12292
  15.9 76.8 %copy-start.2 = (bf16[128,2048]{1,0:T(8,128)(2,1)S(1)}, bf16[128,2048]{1,0:T(8,128)(2,1)}, u32[]{:S(2)}) copy-start(bf16[128,2048]{1,0:T(8,128)(2,1)} %param.15) | copy-start | bytes 1572868
  15.9 5.3 %collective-permute-start = (bf16[2,128,256]{1,2,0:T(8,128)(2,1)S(1)}, bf16[2,128,256]{1,2,0:T(8,128)(2,1)S(1)}, u32[]{:S(2)}, u32[]{:S(2)}) collective-permute-start(bf16[2,128,256]{1,2,0:T(8,128)(2,1)S(1)} %get-tuple-element.499), channel_id=1, source_target_pairs={{0,4},{1,5},{2,6},{3,7},{4,8},{5,9},{6,10},{7,11},{8,12},{9,13},{1... | collective-permute-start | bytes 393224 | tf_op jit(solution)/shard_map/while/body/eval_jaxpr/ppermute | solution.py:21
  23.9 8.3 %collective-permute-start = (bf16[2,128,256]{1,2,0:T(8,128)(2,1)S(1)}, bf16[2,128,256]{1,2,0:T(8,128)(2,1)S(1)}, u32[]{:S(2)}, u32[]{:S(2)}) collective-permute-start(bf16[2,128,256]{1,2,0:T(8,128)(2,1)S(1)} %get-tuple-element.499), channel_id=1, source_target_pairs={{0,4},{1,5},{2,6},{3,7},{4,8},{5,9},{6,10},{7,11},{8,12},{9,13},{1... | collective-permute-start | bytes 393224 | tf_op jit(solution)/shard_map/while/body/eval_jaxpr/ppermute | solution.py:21
  35.0 8.5 %collective-permute-start = (bf16[2,128,256]{1,2,0:T(8,128)(2,1)S(1)}, bf16[2,128,256]{1,2,0:T(8,128)(2,1)S(1)}, u32[]{:S(2)}, u32[]{:S(2)}) collective-permute-start(bf16[2,128,256]{1,2,0:T(8,128)(2,1)S(1)} %get-tuple-element.499), channel_id=1, source_target_pairs={{0,4},{1,5},{2,6},{3,7},{4,8},{5,9},{6,10},{7,11},{8,12},{9,13},{1... | collective-permute-start | bytes 393224 | tf_op jit(solution)/shard_map/while/body/eval_jaxpr/ppermute | solution.py:21
  44.4 54.2 %copy-start.1 = (bf16[16,8,16,128]{3,1,2,0:T(8,128)(2,1)}, bf16[16,8,16,128]{3,1,2,0:T(8,128)(2,1)S(1)}, u32[]{:S(2)}) copy-start(bf16[16,8,16,128]{3,1,2,0:T(8,128)(2,1)S(1)} %copy.58) | copy-start | bytes 1572868
  44.4 53.1 %copy-start.4 = (f32[2048]{0:T(1024)S(1)}, f32[2048]{0:T(1024)}, u32[]{:S(2)}) copy-start(f32[2048]{0:T(1024)} %param.23) | copy-start | bytes 24580
  97.5 1.2 copy-start
Sparse Core Ops, SparseCore 0:
  10.1 82.4 all-gather.2

commit v2 on v1

--- a/solution.py
+++ b/solution.py
@@ -22,15 +22,16 @@
 
 
 VMEM_BYTES = 60 * 2**20
-
-
-def put(src, dst, send_sem, recv_sem, to):
+HALVES = 2
+
+
+def put(src, dst, send_sem, recv_sem, to, axis="ctx"):
     return pltpu.make_async_remote_copy(
         src_ref=src,
         dst_ref=dst,
         send_sem=send_sem,
         recv_sem=recv_sem,
-        device_id={"ctx": to},
+        device_id={axis: to},
         device_id_type=pl.DeviceIdType.MESH,
     )
 
@@ -42,15 +43,26 @@
     return z + sign * jnp.where(step <= 2 * short, near, step - short)
 
 
-def expert_kernel(
+def layer_kernel(
     planes,
     cap,
-    normed_ref,
-    updated_ref,
-    gates_ref,
+    order_ref,
+    residual_ref,
+    queries_ref,
+    keys_ref,
+    values_ref,
+    table_ref,
+    gain_ref,
+    weight_ref,
     up_hbm,
     down_hbm,
+    context_ref,
     out_ref,
+    kv,
+    tables,
+    gates_ref,
+    columns,
+    updated_ref,
     rows_all,
     contrib,
     from_core,
@@ -61,6 +73,16 @@
     ranks,
     picked,
     act,
+    kv_s,
+    kv_r,
+    t_s,
+    t_r,
+    o_recv,
+    o_up_s,
+    o_dn_s,
+    o_y_s,
+    o_x_s,
+    o_c_s,
     w_sem,
     recv,
     up_s,
@@ -74,7 +96,7 @@
     rz_s,
     rz_r,
 ):
-    n, width = normed_ref.shape
+    n, width = residual_ref.shape
     hidden = w_down.shape[0]
     pair = 2 * n
     me = lax.axis_index("ctx")
@@ -94,17 +116,174 @@
 
     barrier = pltpu.get_barrier_semaphore()
 
-    def greet(to):
+    def greet(to, axis="ctx"):
         pl.semaphore_signal(
-            barrier, inc=1, device_id={"ctx": to}, device_id_type=pl.DeviceIdType.MESH
-        )
-
+            barrier, inc=1, device_id={axis: to}, device_id_type=pl.DeviceIdType.MESH
+        )
+
+    group = lax.axis_index("groups")
+    at_x = 1 - group
+    experts = planes * SEQS
+    greet(at_x, "groups")
     greet(at_y)
     greet(at_core)
-    pl.when(above)(lambda: greet(me + SEQS))
-    pl.when(below)(lambda: greet(me - SEQS))
-    block(rows_all, me)[...] = normed_ref[...]
-    pl.semaphore_wait(barrier, 2 + jnp.where(above, 1, 0) + jnp.where(below, 1, 0))
+    for by in range(1, planes):
+        greet(lax.rem(z + by, planes) * SEQS + place)
+    kv_width = keys_ref.shape[1]
+    own_kv = block(kv, z)
+    own_kv[:, :kv_width] = keys_ref[...]
+    own_kv[:, kv_width:] = values_ref[...]
+    column = c * 2 + y
+
+    def table(col, plane, count):
+        start = pl.multiple_of((col * planes + plane) * experts, experts)
+        return tables.at[pl.ds(start, count * experts)]
+
+    table(column, z, 1)[...] = table_ref[...]
+    columns[me] = weight_ref[...]
+    pl.semaphore_wait(barrier, planes + 2)
+
+    def kv_copy(plane, by):
+        return put(block(kv, plane), block(kv, plane), kv_s.at[by], kv_r.at[plane], at_y)
+
+    def send_kv(by):
+        to = lax.rem(z + by, planes) * SEQS + place
+        return (
+            put(own_kv, own_kv, kv_s.at[by], kv_r.at[z], to),
+            put(table(column, z, 1), table(column, z, 1), t_s.at[by], t_r.at[z], to),
+        )
+
+    def tables_to_y():
+        part = table(column, 0, planes)
+        return put(part, part, t_s.at[planes], t_r.at[planes], at_y)
+
+    def tables_to_core():
+        part = table(c * 2, 0, 2 * planes)
+        return put(part, part, t_s.at[planes + 1], t_r.at[planes + 1], at_core)
+
+    for by in range(1, planes):
+        for copy in send_kv(by):
+            copy.start()
+
+    def column_copy(index, sem, to, axis="ctx"):
+        return put(columns.at[index], columns.at[index], sem, o_recv.at[index], to, axis)
+
+    def column_forwards(p):
+        index = p * SEQS + place
+        return (
+            (above & (p <= z), column_copy(index, o_up_s.at[p], me + SEQS)),
+            (below & (p >= z), column_copy(index, o_dn_s.at[p], me - SEQS)),
+            (c == group, column_copy(index, o_y_s.at[p], at_y)),
+            (None, column_copy(index, o_c_s.at[p * 2 + y], at_core)),
+        )
+
+    def column_seconds(p):
+        index = p * SEQS + (1 - y) * 2 + c
+        return (
+            (c == group, column_copy(index, o_x_s.at[p], at_x, "groups")),
+            (None, column_copy(index, o_c_s.at[p * 2 + 1 - y], at_core)),
+        )
+
+    def start_all(copies):
+        for condition, copy in copies:
+            if condition is None:
+                copy.start()
+            else:
+                pl.when(condition)(copy.start)
+
+    def sent_all(copies):
+        for condition, copy in copies:
+            if condition is None:
+                copy.wait_send()
+            else:
+                pl.when(condition)(copy.wait_send)
+
+    start_all(column_forwards(z))
+    for by in range(1, planes):
+        plane = lax.rem(z + by, planes)
+        kv_copy(plane, by).wait_recv()
+        put(
+            table(column, plane, 1), table(column, plane, 1), t_s.at[by], t_r.at[plane], at_y
+        ).wait_recv()
+    tables_to_y().start()
+
+    total_keys = planes * n
+    lane = lax.broadcasted_iota(jnp.int32, (n, total_keys), 1)
+    key_plane = lane // n
+    key_position = lane % n
+    for plane in range(planes):
+        key_position = key_position + jnp.where(
+            key_plane == plane, order_ref[plane * SEQS + place] * n, 0
+        )
+    query_position = order_ref[me] * n + lax.broadcasted_iota(jnp.int32, (n, total_keys), 0)
+    visible = key_position <= query_position
+    heads = width // HEAD_SIZE
+    kv_heads = kv_width // HEAD_SIZE
+
+    def attend(head, carry):
+        cols = pl.ds(pl.multiple_of(head * HEAD_SIZE, HEAD_SIZE), HEAD_SIZE)
+        kv_head = head // (heads // kv_heads)
+        key_cols = pl.ds(pl.multiple_of(kv_head * HEAD_SIZE, HEAD_SIZE), HEAD_SIZE)
+        value_cols = pl.ds(pl.multiple_of(kv_width + kv_head * HEAD_SIZE, HEAD_SIZE), HEAD_SIZE)
+        scores = lax.dot_general(
+            queries_ref[:, cols],
+            kv[:, key_cols],
+            (((1,), (1,)), ((), ())),
+            preferred_element_type=jnp.float32,
+        ) * (HEAD_SIZE**-0.5)
+        scores = jnp.where(visible, scores, -jnp.inf)
+        weights = jnp.exp(scores - jnp.max(scores, axis=1, keepdims=True))
+        total = jnp.sum(weights, axis=1, keepdims=True)
+        summed = jnp.dot(
+            weights.astype(jnp.bfloat16), kv[:, value_cols], preferred_element_type=jnp.float32
+        )
+        context_ref[:, cols] = (summed / total).astype(jnp.bfloat16)
+        return carry
+
+    lax.fori_loop(0, heads, attend, 0, unroll=4)
+    tables_to_y().wait_recv()
+    tables_to_core().start()
+
+    def weight_step(k, carry):
+        @pl.when(k < planes)
+        def _():
+            p = plane_at(k, z, planes)
+            column_copy(p * SEQS + place, o_y_s.at[p], at_y).wait_recv()
+            start_all(column_forwards(p))
+
+        p = plane_at(k - 1, z, planes)
+        column_copy(p * SEQS + (1 - y) * 2 + c, o_y_s.at[p], at_y).wait_recv()
+        start_all(column_seconds(p))
+        for row in range(2):
+            column_copy(p * SEQS + row * 2 + 1 - c, o_y_s.at[p], at_core).wait_recv()
+        for spot in range(SEQS):
+            index = p * SEQS + spot
+            each = columns.shape[2]
+            cols = pl.ds(pl.multiple_of(index * each, each), each)
+            updated_ref[:, cols] = residual_ref[:, cols].astype(jnp.float32) + jnp.dot(
+                context_ref[...], columns[index], preferred_element_type=jnp.float32
+            )
+        return carry
+
+    lax.fori_loop(1, planes + 1, weight_step, 0)
+    tables_to_core().wait_recv()
+
+    def norm(i, carry):
+        rows = pl.ds(pl.multiple_of(i * 16, 16), 16)
+        rows_there = pl.ds(pl.multiple_of(me * n + i * 16, 16), 16)
+        updated = updated_ref[rows, :]
+        mean = jnp.mean(updated * updated, axis=1, keepdims=True)
+        rows_all[rows_there, :] = (updated * lax.rsqrt(mean + 1e-06) * gain_ref[...]).astype(
+            jnp.bfloat16
+        )
+        return carry
+
+    lax.fori_loop(0, n // 16, norm, 0)
+    for p in range(planes):
+        for row in range(2):
+            for core in range(2):
+                at = ((core * 2 + row) * planes + p) * experts + me
+                gates_ref[pl.ds(p * 2 + row, 1), pl.ds(core * n, n)] = tables[pl.ds(at, 1), :]
 
     def gather_copy(index, sem, to):
         return put(block(rows_all, index), block(rows_all, index), sem, recv.at[index], to)
@@ -130,18 +309,28 @@
             at_core,
         )
 
-    def y_return(p):
+    small = n // HALVES
+
+    def piece(ref, index, h):
+        return ref.at[pl.ds(pl.multiple_of(index * n + h * small, small), small)]
+
+    def y_return(p, h):
+        at = p * HALVES + h
         return put(
-            block(contrib, p * SEQS + (1 - y) * 2 + c),
-            block(from_y, p),
-            ry_s.at[p],
-            ry_r.at[p],
+            piece(contrib, p * SEQS + (1 - y) * 2 + c, h),
+            piece(from_y, p, h),
+            ry_s.at[at],
+            ry_r.at[at],
             at_y,
         )
 
-    def z_return(p, slot, to):
+    def z_return(p, slot, h, to):
         return put(
-            block(contrib, p * SEQS + place), block(from_z, slot), rz_s.at[p], rz_r.at[slot], to
+            piece(contrib, p * SEQS + place, h),
+            piece(from_z, slot, h),
+            rz_s.at[p * HALVES + h],
+            rz_r.at[slot * HALVES + h],
+            to,
         )
 
     shape = (pair, pair)
@@ -216,11 +405,7 @@
             def _():
                 gather_copy(p * SEQS + place, y_s.at[p], at_y).wait_recv()
 
-            for condition, copy in forwards(p):
-                if condition is None:
-                    copy.start()
-                else:
-                    pl.when(condition)(copy.start)
+            start_all(forwards(p))
 
         @pl.when(k > 0)
         def _():
@@ -253,81 +438,114 @@
             target[here, :] = total.astype(target.dtype)
             return carry
 
-        lax.fori_loop(0, n // chunk, some, 0)
+        lax.fori_loop(0, small // chunk, some, 0)
 
     def core_sum(i, carry):
         p = plane_at(planes - 1 - i, z, planes)
         for row in range(2):
             core_return(p, row).wait_recv()
-        other = block(contrib, p * SEQS + (1 - y) * 2 + c)
-        add_up(other, [other, block(from_core, p * 2 + 1 - y)])
-        y_return(p).start()
+        for h in range(HALVES):
+            other = piece(contrib, p * SEQS + (1 - y) * 2 + c, h)
+            add_up(other, [other, piece(from_core, p * 2 + 1 - y, h)])
+            y_return(p, h).start()
         return carry
 
     lax.fori_loop(0, planes, core_sum, 0)
 
     def chain(i, carry):
-        p = plane_at(planes - 1 - i, z, planes)
-        y_return(p).wait_recv()
-        own = block(contrib, p * SEQS + place)
-        add_up(own, [own, block(from_core, p * 2 + y), block(from_y, p)])
-
-        @pl.when(((p < z) & above) | ((p > z) & below))
+        p = plane_at(planes - 1 - i // HALVES, z, planes)
+        h = i % HALVES
+        y_return(p, h).wait_recv()
+        own = piece(contrib, p * SEQS + place, h)
+        terms = [own, piece(from_core, p * 2 + y, h), piece(from_y, p, h)]
+        onward = ((p < z) & above) | ((p > z) & below)
+
+        @pl.when(onward)
         def _():
-            z_return(p, p, at_y).wait_recv()
-            add_up(own, [own, block(from_z, p)])
+            z_return(p, p, h, at_y).wait_recv()
+            add_up(own, terms + [piece(from_z, p, h)])
+
+        pl.when(jnp.logical_not(onward))(lambda: add_up(own, terms))
 
         @pl.when(p < z)
         def _():
-            z_return(p, jnp.where(p == z - 1, planes, p), me - SEQS).start()
+            z_return(p, jnp.where(p == z - 1, planes, p), h, me - SEQS).start()
 
         @pl.when(p > z)
         def _():
-            z_return(p, p, me + SEQS).start()
+            z_return(p, p, h, me + SEQS).start()
 
         return carry
 
-    lax.fori_loop(0, planes - 1, chain, 0)
-    y_return(z).wait_recv()
-    mine = block(contrib, me)
-    terms = [updated_ref, mine, block(from_core, z * 2 + y), block(from_y, z)]
-    low, high = block(from_z, z), block(from_z, planes)
-    pl.when(below)(lambda: z_return(z, z, at_y).wait_recv())
-    pl.when(above)(lambda: z_return(z, planes, at_y).wait_recv())
-    pl.when(below & above)(lambda: add_up(out_ref, terms + [low, high]))
-    pl.when(below & jnp.logical_not(above))(lambda: add_up(out_ref, terms + [low]))
-    pl.when(jnp.logical_not(below) & above)(lambda: add_up(out_ref, terms + [high]))
+    lax.fori_loop(0, (planes - 1) * HALVES, chain, 0)
+
+    def last(h, carry):
+        y_return(z, h).wait_recv()
+        result = piece(out_ref, 0, h)
+        terms = [
+            piece(updated_ref, 0, h),
+            piece(contrib, me, h),
+            piece(from_core, z * 2 + y, h),
+            piece(from_y, z, h),
+        ]
+        low, high = piece(from_z, z, h), piece(from_z, planes, h)
+        pl.when(below)(lambda: z_return(z, z, h, at_y).wait_recv())
+        pl.when(above)(lambda: z_return(z, planes, h, at_y).wait_recv())
+        pl.when(below & above)(lambda: add_up(result, terms + [low, high]))
+        pl.when(below & jnp.logical_not(above))(lambda: add_up(result, terms + [low]))
+        pl.when(jnp.logical_not(below) & above)(lambda: add_up(result, terms + [high]))
+        return carry
+
+    lax.fori_loop(0, HALVES, last, 0)
+
+    for by in range(1, planes):
+        for copy in send_kv(by):
+            copy.wait_send()
+    tables_to_y().wait_send()
+    tables_to_core().wait_send()
 
     def finish(p, carry):
-        for condition, copy in forwards(p):
-            if condition is None:
-                copy.wait_send()
-            else:
-                pl.when(condition)(copy.wait_send)
+        sent_all(column_forwards(p))
+        sent_all(column_seconds(p))
+        sent_all(forwards(p))
         second_forward(p).wait_send()
         for row in range(2):
             core_return(p, row).wait_send()
-        y_return(p).wait_send()
-        pl.when(p != z)(lambda: z_return(p, p, at_y).wait_send())
+        for h in range(HALVES):
+            y_return(p, h).wait_send()
+
+        @pl.when(p != z)
+        def _():
+            for h in range(HALVES):
+                z_return(p, p, h, at_y).wait_send()
+
         return carry
 
     lax.fori_loop(0, planes, finish, 0)
 
 
-def expert_call(normed, updated, gates_here, w_gate_up, w_down, cap):
-    n, width = normed.shape
+def layer_call(
+    order, residual, queries, keys, values, table, gain, out_weight, w_gate_up, w_down, cap
+):
+    n, width = residual.shape
     hidden = w_down.shape[1]
     devices = lax.axis_size("ctx")
     planes = devices // SEQS
     vmem = pl.BlockSpec(memory_space=pltpu.VMEM)
     anywhere = pl.BlockSpec(memory_space=pl.ANY)
     bf16 = jnp.bfloat16
+    dma = pltpu.SemaphoreType.DMA
     return pl.pallas_call(
-        functools.partial(expert_kernel, planes, cap),
-        out_shape=jax.ShapeDtypeStruct((n, width), bf16),
-        in_specs=[vmem, vmem, vmem, anywhere, anywhere],
-        out_specs=vmem,
+        functools.partial(layer_kernel, planes, cap),
+        out_shape=[jax.ShapeDtypeStruct((n, width), bf16)] * 2,
+        in_specs=[pl.BlockSpec(memory_space=pltpu.SMEM)] + [vmem] * 7 + [anywhere] * 2,
+        out_specs=[vmem, vmem],
         scratch_shapes=[
+            pltpu.VMEM((planes * n, 2 * keys.shape[1]), bf16),
+            pltpu.VMEM((devices * devices, n), jnp.float32),
+            pltpu.VMEM((2 * planes, 2 * n), jnp.float32),
+            pltpu.VMEM((devices,) + out_weight.shape, bf16),
+            pltpu.VMEM((n, width), jnp.float32),
             pltpu.VMEM((devices * n, width), bf16),
             pltpu.VMEM((devices * n, width), bf16),
             pltpu.VMEM((2 * planes * n, width), bf16),
@@ -338,38 +556,45 @@
             pltpu.VMEM((2 * planes, 2 * n), jnp.int32),
             pltpu.VMEM((SEQS * cap, width), bf16),
             pltpu.VMEM((SEQS * cap, hidden), bf16),
-            pltpu.SemaphoreType.DMA((2,)),
-            pltpu.SemaphoreType.DMA((devices,)),
-            pltpu.SemaphoreType.DMA((planes,)),
-            pltpu.SemaphoreType.DMA((planes,)),
-            pltpu.SemaphoreType.DMA((planes,)),
-            pltpu.SemaphoreType.DMA((2 * planes,)),
-            pltpu.SemaphoreType.DMA((2 * planes,)),
-            pltpu.SemaphoreType.DMA((2 * planes,)),
-            pltpu.SemaphoreType.DMA((planes,)),
-            pltpu.SemaphoreType.DMA((planes,)),
-            pltpu.SemaphoreType.DMA((planes,)),
-            pltpu.SemaphoreType.DMA((planes + 1,)),
+            dma((planes,)),
+            dma((planes,)),
+            dma((planes + 2,)),
+            dma((planes + 2,)),
+            dma((devices,)),
+            dma((planes,)),
+            dma((planes,)),
+            dma((planes,)),
+            dma((planes,)),
+            dma((2 * planes,)),
+            dma((2,)),
+            dma((devices,)),
+            dma((planes,)),
+            dma((planes,)),
+            dma((planes,)),
+            dma((2 * planes,)),
+            dma((2 * planes,)),
+            dma((2 * planes,)),
+            dma((HALVES * planes,)),
+            dma((HALVES * planes,)),
+            dma((HALVES * planes,)),
+            dma((HALVES * (planes + 1),)),
         ],
         compiler_params=pltpu.CompilerParams(
             collective_id=0, has_side_effects=True, vmem_limit_bytes=VMEM_BYTES
         ),
-        name="experts",
-    )(normed, updated, gates_here, w_gate_up, w_down)
-
-
-def gates_for_own(routes, route_weights, devices):
+        name="layer",
+    )(order, residual, queries, keys, values, table, gain, out_weight, w_gate_up, w_down)
+
+
+def gate_table(routes, route_weights, experts):
     gates = route_weights / jnp.sum(route_weights, axis=-1, keepdims=True)
-    chosen = routes.T[None] == jnp.arange(devices, dtype=jnp.int32)[:, None, None]
-    table = jnp.sum(jnp.where(chosen, gates.T[None], 0.0), axis=1)
-    everyone = lax.all_gather(table, "ctx", axis=0)
-    mine = lax.dynamic_index_in_dim(everyone, lax.axis_index("ctx"), axis=1, keepdims=False)
-    return mine.reshape(devices // 2, 2 * routes.shape[0])
+    chosen = routes.T[None] == jnp.arange(experts, dtype=jnp.int32)[:, None, None]
+    return jnp.sum(jnp.where(chosen, gates.T[None], 0.0), axis=1)
 
 
 def fits(devices, rows, width, hidden):
-    blocks = 3 * devices + 4
-    return 2 * (blocks * rows * width + 3 * width * hidden) < VMEM_BYTES * 4 // 5
+    blocks = 4 * devices + 8
+    return lax.axis_size("groups") == 2 and 2 * (blocks * rows * width + 3 * width * hidden) < VMEM_BYTES * 4 // 5
 
 
 def local(
@@ -390,8 +615,25 @@
     devices = lax.axis_size("ctx")
     cycle_length = devices // SEQS
     own_index = lax.axis_index("ctx")
+    experts = devices * w_gate_up.shape[0]
+    capacity = 9 * device_row_count * TOPK // (8 * experts)
+    if fits(devices, device_row_count, D, FF):
+        return tuple(
+            layer_call(
+                block_order,
+                residual,
+                queries,
+                keys,
+                values,
+                gate_table(routes, route_weights, experts),
+                norm_gain.reshape(1, -1),
+                out_weight,
+                w_gate_up,
+                w_down,
+                capacity,
+            )
+        )
     full_weight = lax.all_gather(out_weight, "ctx", axis=1, tiled=True)
-    gates_here = gates_for_own(routes, route_weights, devices)
     query_position = block_order[own_index]
     query_head_rows = (
         queries.reshape(device_row_count, KEY_VALUE_HEADS, query_group_width, HEAD_SIZE)
@@ -466,9 +708,6 @@
     ).astype(jnp.bfloat16)
     experts = devices * w_gate_up.shape[0]
     capacity = 9 * device_row_count * TOPK // (8 * experts)
-    if fits(devices, device_row_count, D, FF):
-        mixed = expert_call(normed, updated, gates_here, w_gate_up, w_down, capacity)
-        return (context, mixed)
     expert_ids = routes.reshape(-1)
     one_hot = (expert_ids[:, None] == jnp.arange(experts, dtype=jnp.int32)[None, :]).astype(
         jnp.int32

time: 235 us -> 203 us (0.86)
  the two profiles are of different devices: /device:TPU:10 before, /device:TPU:2 now
where the time goes in v2:
time: 203 us
  Pallas kernels  196 us (97%)
  local copies, waits for them, and re-layouts  3.76 us (2%)
  other arithmetic  2.7 us (1%)
    pallas_call x1, Pallas kernels, layer_call(): pl.pallas_call(functools.partial(layer_kernel, planes, cap), out_shape=[j...  196 us

profile of v2, /device:TPU:2, one launch (start us, length us, event | category | flops | bytes accessed | tf_op | source)
XLA Modules:
  0.0 202.7 jit_solution(7110997568364867361)
XLA Ops:
  0.6 0.7 reduce_sum.18
  1.3 0.7 divide_bitcast_fusion
  2.0 1.3 select_reduce_fusion.table_ref
  3.3 195.6 %layer.1 = (bf16[128,2048]{1,0:T(8,128)(2,1)}, bf16[128,2048]{1,0:T(8,128)(2,1)}) custom-call(s32[16]{0:T(128)} %order_ref.1, bf16[128,2048]{1,0:T(8,128)(2,1)} %residual_ref.1, bf16[128,2048]{1,0:T(8,128)(2,1)} %queries_ref.1, bf16[128,256]{1,0:T(8,128)(2,1)} %keys_ref.1, bf16[128,256]{1,0:T(8,128)(2,1)} %values_ref.1, ...), custom_call_target="tpu_custom_call" | custom-call | tf_op jit(solution)/shard_map/layer/pallas_call | solution.py:538
  198.9 1.9 copy.15
  200.8 1.9 copy.16

commit v3 on v2

--- a/solution.py
+++ b/solution.py
@@ -180,8 +180,8 @@
     def column_seconds(p):
         index = p * SEQS + (1 - y) * 2 + c
         return (
-            (c == group, column_copy(index, o_x_s.at[p], at_x, "groups")),
-            (None, column_copy(index, o_c_s.at[p * 2 + 1 - y], at_core)),
+            column_copy(index, o_x_s.at[p], at_x, "groups"),
+            column_copy(index, o_c_s.at[p * 2 + 1 - y], at_core),
         )
 
     def start_all(copies):
@@ -251,21 +251,35 @@
             column_copy(p * SEQS + place, o_y_s.at[p], at_y).wait_recv()
             start_all(column_forwards(p))
 
-        p = plane_at(k - 1, z, planes)
-        column_copy(p * SEQS + (1 - y) * 2 + c, o_y_s.at[p], at_y).wait_recv()
-        start_all(column_seconds(p))
-        for row in range(2):
-            column_copy(p * SEQS + row * 2 + 1 - c, o_y_s.at[p], at_core).wait_recv()
-        for spot in range(SEQS):
-            index = p * SEQS + spot
-            each = columns.shape[2]
-            cols = pl.ds(pl.multiple_of(index * each, each), each)
-            updated_ref[:, cols] = residual_ref[:, cols].astype(jnp.float32) + jnp.dot(
-                context_ref[...], columns[index], preferred_element_type=jnp.float32
-            )
+        @pl.when((k <= planes) & (c == group))
+        def _():
+            p = plane_at(k - 1, z, planes)
+            column_copy(p * SEQS + (1 - y) * 2 + c, o_y_s.at[p], at_y).wait_recv()
+            for copy in column_seconds(p):
+                copy.start()
+
+        @pl.when(k > 1)
+        def _():
+            p = plane_at(k - 2, z, planes)
+
+            @pl.when(c != group)
+            def _():
+                column_copy(p * SEQS + (1 - y) * 2 + c, o_y_s.at[p], at_y).wait_recv()
+                column_seconds(p)[1].start()
+
+            for row in range(2):
+                column_copy(p * SEQS + row * 2 + 1 - c, o_y_s.at[p], at_core).wait_recv()
+            for spot in range(SEQS):
+                index = p * SEQS + spot
+                each = columns.shape[2]
+                cols = pl.ds(pl.multiple_of(index * each, each), each)
+                updated_ref[:, cols] = residual_ref[:, cols].astype(jnp.float32) + jnp.dot(
+                    context_ref[...], columns[index], preferred_element_type=jnp.float32
+                )
+
         return carry
 
-    lax.fori_loop(1, planes + 1, weight_step, 0)
+    lax.fori_loop(1, planes + 2, weight_step, 0)
     tables_to_core().wait_recv()
 
     def norm(i, carry):
@@ -378,17 +392,14 @@
 
         def down(j, carry):
             cols = pl.ds(pl.multiple_of(j * tile, tile), tile)
+            result = jnp.dot(act[...], w_down[:, cols], preferred_element_type=jnp.float32)
             for half in range(2):
                 choose, gate = parts[half]
                 source = pl.ds(pl.multiple_of((p * 2 + half) * pair, pair), pair)
-                result = jnp.dot(
-                    act[pl.ds(half * 2 * cap, 2 * cap), :],
-                    w_down[:, cols],
-                    preferred_element_type=jnp.float32,
-                )
+                part = result[half * 2 * cap : (half + 1) * 2 * cap] * gate
                 contrib[source, cols] = lax.dot_general(
                     choose,
-                    (result * gate).astype(jnp.bfloat16),
+                    part.astype(jnp.bfloat16),
                     (((0,), (0,)), ((), ())),
                     preferred_element_type=jnp.float32,
                 ).astype(jnp.bfloat16)
@@ -396,37 +407,6 @@
 
         lax.fori_loop(0, width // tile, down, 0)
 
-    def advance(k, carry):
-        @pl.when(k < planes)
-        def _():
-            p = plane_at(k, z, planes)
-
-            @pl.when(k > 0)
-            def _():
-                gather_copy(p * SEQS + place, y_s.at[p], at_y).wait_recv()
-
-            start_all(forwards(p))
-
-        @pl.when(k > 0)
-        def _():
-            p = plane_at(k - 1, z, planes)
-            second_forward(p).wait_recv()
-            second_forward(p).start()
-            for row in range(2):
-                gather_copy(p * SEQS + row * 2 + 1 - c, c_s.at[0], at_core).wait_recv()
-
-            @pl.when(k == 1)
-            def _():
-                load_up.wait()
-                load_down.wait()
-
-            compute(p)
-            for row in range(2):
-                core_return(p, row).start()
-
-        return carry
-
-    lax.fori_loop(0, planes + 1, advance, 0)
     chunk = 16
 
     def add_up(target, terms):
@@ -440,17 +420,54 @@
 
         lax.fori_loop(0, small // chunk, some, 0)
 
-    def core_sum(i, carry):
-        p = plane_at(planes - 1 - i, z, planes)
+    def core_sum(p):
         for row in range(2):
             core_return(p, row).wait_recv()
         for h in range(HALVES):
             other = piece(contrib, p * SEQS + (1 - y) * 2 + c, h)
             add_up(other, [other, piece(from_core, p * 2 + 1 - y, h)])
             y_return(p, h).start()
+
+    def advance(k, carry):
+        @pl.when(k < planes)
+        def _():
+            p = plane_at(k, z, planes)
+
+            @pl.when(k > 0)
+            def _():
+                gather_copy(p * SEQS + place, y_s.at[p], at_y).wait_recv()
+
+            start_all(forwards(p))
+
+        j = k - lag
+
+        @pl.when((j >= 0) & (j < planes))
+        def _():
+            p = plane_at(j, z, planes)
+            second_forward(p).wait_recv()
+            second_forward(p).start()
+            pl.when(j == planes - 1)(lambda: core_sum(z))
+            for row in range(2):
+                gather_copy(p * SEQS + row * 2 + 1 - c, c_s.at[0], at_core).wait_recv()
+
+            @pl.when(j == 0)
+            def _():
+                load_up.wait()
+                load_down.wait()
+
+            compute(p)
+            for row in range(2):
+                core_return(p, row).start()
+
         return carry
 
-    lax.fori_loop(0, planes, core_sum, 0)
+    lag = 1 + jnp.where(above & below, 1, 0)
+    lax.fori_loop(0, planes + 2, advance, 0)
+    def far_sum(i, carry):
+        core_sum(plane_at(planes - 1 - i, z, planes))
+        return carry
+
+    lax.fori_loop(0, planes - 1, far_sum, 0)
 
     def chain(i, carry):
         p = plane_at(planes - 1 - i // HALVES, z, planes)
@@ -506,7 +523,8 @@
 
     def finish(p, carry):
         sent_all(column_forwards(p))
-        sent_all(column_seconds(p))
+        pl.when(c == group)(column_seconds(p)[0].wait_send)
+        column_seconds(p)[1].wait_send()
         sent_all(forwards(p))
         second_forward(p).wait_send()
         for row in range(2):

time: 203 us -> 186 us (0.916)
  the two profiles are of different devices: /device:TPU:2 before, /device:TPU:10 now
where the time goes in v3:
time: 186 us; the launch traced here: 185 us
  Pallas kernels  178 us (96%)
  local copies, waits for them, and re-layouts  3.76 us (2%)
  other arithmetic  2.7 us (1%)
    pallas_call x1, Pallas kernels, layer_call(): pl.pallas_call(functools.partial(layer_kernel, planes, cap), out_shape=[j...  178 us
    unnamed x2, local copies, waits for them, and re-layouts  3.76 us

profile of v3, /device:TPU:10, one launch (start us, length us, event | category | flops | bytes accessed | tf_op | source)
XLA Modules:
  0.0 185.2 jit_solution(4910165712031934331)
XLA Ops:
  0.6 0.7 reduce_sum.18
  1.3 0.7 divide_bitcast_fusion
  2.0 1.3 select_reduce_fusion.table_ref
  3.3 178.1 %layer.1 = (bf16[128,2048]{1,0:T(8,128)(2,1)}, bf16[128,2048]{1,0:T(8,128)(2,1)}) custom-call(s32[16]{0:T(128)} %order_ref.1, bf16[128,2048]{1,0:T(8,128)(2,1)} %residual_ref.1, bf16[128,2048]{1,0:T(8,128)(2,1)} %queries_ref.1, bf16[128,256]{1,0:T(8,128)(2,1)} %keys_ref.1, bf16[128,256]{1,0:T(8,128)(2,1)} %values_ref.1, ...), custom_call_target="tpu_custom_call" | custom-call | tf_op jit(solution)/shard_map/layer/pallas_call | solution.py:556
  181.4 1.9 %copy.15 = bf16[128,2048]{1,0:T(8,128)(2,1)} copy(bf16[128,2048]{1,0:T(8,128)(2,1)} %get-tuple-element.4) | data formatting | bytes 1048576
  183.3 1.9 %copy.16 = bf16[128,2048]{1,0:T(8,128)(2,1)} copy(bf16[128,2048]{1,0:T(8,128)(2,1)} %get-tuple-element.5) | data formatting | bytes 1048576

commit v4 on v3

--- a/solution.py
+++ b/solution.py
@@ -22,7 +22,7 @@
 
 
 VMEM_BYTES = 60 * 2**20
-HALVES = 2
+HALVES = 4
 
 
 def put(src, dst, send_sem, recv_sem, to, axis="ctx"):
@@ -51,7 +51,8 @@
     queries_ref,
     keys_ref,
     values_ref,
-    table_ref,
+    routes_ref,
+    shares_ref,
     gain_ref,
     weight_ref,
     up_hbm,
@@ -83,6 +84,7 @@
     o_y_s,
     o_x_s,
     o_c_s,
+    o_far_s,
     w_sem,
     recv,
     up_s,
@@ -139,7 +141,15 @@
         start = pl.multiple_of((col * planes + plane) * experts, experts)
         return tables.at[pl.ds(start, count * experts)]
 
-    table(column, z, 1)[...] = table_ref[...]
+    shares = shares_ref[...]
+    gates = shares / jnp.sum(shares, axis=1, keepdims=True)
+    expert_lane = lax.broadcasted_iota(jnp.int32, (n, HEAD_SIZE), 1)
+    spread = jnp.zeros((n, HEAD_SIZE), jnp.float32)
+    for slot in range(shares_ref.shape[1]):
+        spread = spread + jnp.where(
+            routes_ref[:, slot : slot + 1] == expert_lane, gates[:, slot : slot + 1], 0.0
+        )
+    table(column, z, 1)[...] = spread.T[:experts]
     columns[me] = weight_ref[...]
     pl.semaphore_wait(barrier, planes + 2)
 
@@ -170,9 +180,14 @@
 
     def column_forwards(p):
         index = p * SEQS + place
+        keep = c == group
+        up = above & (p <= z) & (keep | (p > 0) | (z + 2 < planes))
+        down = below & (p >= z) & (keep | (p < planes - 1) | (z > 1))
+        ends = ((z == 0) & (p == planes - 1)) | ((z == planes - 1) & (p == 0))
         return (
-            (above & (p <= z), column_copy(index, o_up_s.at[p], me + SEQS)),
-            (below & (p >= z), column_copy(index, o_dn_s.at[p], me - SEQS)),
+            (up, column_copy(index, o_up_s.at[p], me + SEQS)),
+            (down, column_copy(index, o_dn_s.at[p], me - SEQS)),
+            (keep & ends, column_copy(index, o_far_s, at_x, "groups")),
             (c == group, column_copy(index, o_y_s.at[p], at_y)),
             (None, column_copy(index, o_c_s.at[p * 2 + y], at_core)),
         )
@@ -543,7 +558,18 @@
 
 
 def layer_call(
-    order, residual, queries, keys, values, table, gain, out_weight, w_gate_up, w_down, cap
+    order,
+    residual,
+    queries,
+    keys,
+    values,
+    routes,
+    shares,
+    gain,
+    out_weight,
+    w_gate_up,
+    w_down,
+    cap,
 ):
     n, width = residual.shape
     hidden = w_down.shape[1]
@@ -556,7 +582,7 @@
     return pl.pallas_call(
         functools.partial(layer_kernel, planes, cap),
         out_shape=[jax.ShapeDtypeStruct((n, width), bf16)] * 2,
-        in_specs=[pl.BlockSpec(memory_space=pltpu.SMEM)] + [vmem] * 7 + [anywhere] * 2,
+        in_specs=[pl.BlockSpec(memory_space=pltpu.SMEM)] + [vmem] * 8 + [anywhere] * 2,
         out_specs=[vmem, vmem],
         scratch_shapes=[
             pltpu.VMEM((planes * n, 2 * keys.shape[1]), bf16),
@@ -584,6 +610,7 @@
             dma((planes,)),
             dma((planes,)),
             dma((2 * planes,)),
+            dma,
             dma((2,)),
             dma((devices,)),
             dma((planes,)),
@@ -601,13 +628,7 @@
             collective_id=0, has_side_effects=True, vmem_limit_bytes=VMEM_BYTES
         ),
         name="layer",
-    )(order, residual, queries, keys, values, table, gain, out_weight, w_gate_up, w_down)
-
-
-def gate_table(routes, route_weights, experts):
-    gates = route_weights / jnp.sum(route_weights, axis=-1, keepdims=True)
-    chosen = routes.T[None] == jnp.arange(experts, dtype=jnp.int32)[:, None, None]
-    return jnp.sum(jnp.where(chosen, gates.T[None], 0.0), axis=1)
+    )(order, residual, queries, keys, values, routes, shares, gain, out_weight, w_gate_up, w_down)
 
 
 def fits(devices, rows, width, hidden):
@@ -643,7 +664,8 @@
                 queries,
                 keys,
                 values,
-                gate_table(routes, route_weights, experts),
+                routes,
+                route_weights,
                 norm_gain.reshape(1, -1),
                 out_weight,
                 w_gate_up,

time: 186 us -> 184 us (0.989)
  local copies, waits for them, and re-layouts: 3.76 us -> 6.59 us
  other arithmetic: 2.7 us -> 0 us
  Pallas kernels: 178 us -> 176 us
    unnamed x2 -> x4, local copies, waits for them, and re-layouts: 3.76 us -> 6.59 us
    reduce_sum x2 -> x0, other arithmetic: 2.01 us -> none  [the longest x1 1.31 us: gate_table(): return jnp.sum(jnp.where(chosen, gates.T[None], 0.0), axis=1)]
where the time goes in v4:
time: 184 us
  Pallas kernels  176 us (96%)
  local copies, waits for them, and re-layouts  6.59 us (4%)
    pallas_call x1, Pallas kernels, layer_call(): pl.pallas_call(functools.partial(layer_kernel, planes, cap), out_shape=[j...  176 us
    unnamed x4, local copies, waits for them, and re-layouts  6.59 us

profile of v4, /device:TPU:10, one launch (start us, length us, event | category | flops | bytes accessed | tf_op | source)
XLA Modules:
  0.0 183.6 jit_solution(13575243971501207760)
XLA Ops:
  0.6 1.4 copy.13.routes_ref
  2.0 1.4 copy.14.shares_ref
  3.5 176.4 %layer.1 = (bf16[128,2048]{1,0:T(8,128)(2,1)}, bf16[128,2048]{1,0:T(8,128)(2,1)}) custom-call(s32[16]{0:T(128)} %order_ref.1, bf16[128,2048]{1,0:T(8,128)(2,1)} %residual_ref.1, bf16[128,2048]{1,0:T(8,128)(2,1)} %queries_ref.1, bf16[128,256]{1,0:T(8,128)(2,1)} %keys_ref.1, bf16[128,256]{1,0:T(8,128)(2,1)} %values_ref.1, s32[128,8]{1,0:T(8,128)} %copy.13.routes_ref, ...), custom_call_target="tpu_custom_call" | custom-call | tf_op jit(solution)/shard_map/layer/pallas_call | solution.py:582
  179.8 1.9 %copy.17 = bf16[128,2048]{1,0:T(8,128)(2,1)} copy(bf16[128,2048]{1,0:T(8,128)(2,1)} %get-tuple-element.4) | data formatting | bytes 1048576
  181.7 1.9 %copy.18 = bf16[128,2048]{1,0:T(8,128)(2,1)} copy(bf16[128,2048]{1,0:T(8,128)(2,1)} %get-tuple-element.5) | data formatting | bytes 1048576

commit v5 on v4

--- a/solution.py
+++ b/solution.py
@@ -51,8 +51,7 @@
     queries_ref,
     keys_ref,
     values_ref,
-    routes_ref,
-    shares_ref,
+    choices_ref,
     gain_ref,
     weight_ref,
     up_hbm,
@@ -141,13 +140,14 @@
         start = pl.multiple_of((col * planes + plane) * experts, experts)
         return tables.at[pl.ds(start, count * experts)]
 
-    shares = shares_ref[...]
+    slots = choices_ref.shape[1] // 2
+    routes, shares = choices_ref[:, :slots], choices_ref[:, slots:]
     gates = shares / jnp.sum(shares, axis=1, keepdims=True)
-    expert_lane = lax.broadcasted_iota(jnp.int32, (n, HEAD_SIZE), 1)
+    expert_lane = lax.broadcasted_iota(jnp.int32, (n, HEAD_SIZE), 1).astype(jnp.float32)
     spread = jnp.zeros((n, HEAD_SIZE), jnp.float32)
-    for slot in range(shares_ref.shape[1]):
+    for slot in range(slots):
         spread = spread + jnp.where(
-            routes_ref[:, slot : slot + 1] == expert_lane, gates[:, slot : slot + 1], 0.0
+            routes[:, slot : slot + 1] == expert_lane, gates[:, slot : slot + 1], 0.0
         )
     table(column, z, 1)[...] = spread.T[:experts]
     columns[me] = weight_ref[...]
@@ -379,8 +379,8 @@
             row = pl.ds(p * 2 + half, 1)
             hit = lax.broadcasted_iota(jnp.int32, (2 * cap, pair), 0) == ranks[row, :]
             gate = jnp.sum(jnp.where(hit, gates_ref[row, :], 0.0), axis=1, keepdims=True)
-            choose = hit.astype(jnp.float32).astype(jnp.bfloat16)
-            parts.append((choose, gate))
+            chosen = hit.astype(jnp.float32)
+            parts.append((chosen.astype(jnp.bfloat16), chosen.T.astype(jnp.bfloat16), gate))
         tile = 512
 
         def pick(j, carry):
@@ -392,7 +392,7 @@
                 ).astype(jnp.bfloat16)
             return carry
 
-        lax.fori_loop(0, width // tile, pick, 0)
+        lax.fori_loop(0, width // tile, pick, 0, unroll=2)
         narrow = 256
 
         def gate_up(j, carry):
@@ -409,18 +409,15 @@
             cols = pl.ds(pl.multiple_of(j * tile, tile), tile)
             result = jnp.dot(act[...], w_down[:, cols], preferred_element_type=jnp.float32)
             for half in range(2):
-                choose, gate = parts[half]
+                unused, spread_back, gate = parts[half]
                 source = pl.ds(pl.multiple_of((p * 2 + half) * pair, pair), pair)
                 part = result[half * 2 * cap : (half + 1) * 2 * cap] * gate
-                contrib[source, cols] = lax.dot_general(
-                    choose,
-                    part.astype(jnp.bfloat16),
-                    (((0,), (0,)), ((), ())),
-                    preferred_element_type=jnp.float32,
+                contrib[source, cols] = jnp.dot(
+                    spread_back, part.astype(jnp.bfloat16), preferred_element_type=jnp.float32
                 ).astype(jnp.bfloat16)
             return carry
 
-        lax.fori_loop(0, width // tile, down, 0)
+        lax.fori_loop(0, width // tile, down, 0, unroll=2)
 
     chunk = 16
 
@@ -563,8 +560,7 @@
     queries,
     keys,
     values,
-    routes,
-    shares,
+    choices,
     gain,
     out_weight,
     w_gate_up,
@@ -582,7 +578,7 @@
     return pl.pallas_call(
         functools.partial(layer_kernel, planes, cap),
         out_shape=[jax.ShapeDtypeStruct((n, width), bf16)] * 2,
-        in_specs=[pl.BlockSpec(memory_space=pltpu.SMEM)] + [vmem] * 8 + [anywhere] * 2,
+        in_specs=[pl.BlockSpec(memory_space=pltpu.SMEM)] + [vmem] * 7 + [anywhere] * 2,
         out_specs=[vmem, vmem],
         scratch_shapes=[
             pltpu.VMEM((planes * n, 2 * keys.shape[1]), bf16),
@@ -628,7 +624,7 @@
             collective_id=0, has_side_effects=True, vmem_limit_bytes=VMEM_BYTES
         ),
         name="layer",
-    )(order, residual, queries, keys, values, routes, shares, gain, out_weight, w_gate_up, w_down)
+    )(order, residual, queries, keys, values, choices, gain, out_weight, w_gate_up, w_down)
 
 
 def fits(devices, rows, width, hidden):
@@ -664,8 +660,7 @@
                 queries,
                 keys,
                 values,
-                routes,
-                route_weights,
+                jnp.concatenate([routes.astype(jnp.float32), route_weights], axis=1),
                 norm_gain.reshape(1, -1),
                 out_weight,
                 w_gate_up,

time: 184 us -> 183 us (level)
  local copies, waits for them, and re-layouts: 6.59 us -> 4.49 us
    unnamed x4 -> x2, local copies, waits for them, and re-layouts: 6.59 us -> 3.76 us
where the time goes in v5:
time: 183 us
  Pallas kernels  176 us (96%)
  local copies, waits for them, and re-layouts  4.49 us (2%)
    pallas_call x1, Pallas kernels, layer_call(): pl.pallas_call(functools.partial(layer_kernel, planes, cap), out_shape=[j...  176 us
    unnamed x2, local copies, waits for them, and re-layouts  3.76 us

profile of v5, /device:TPU:10, one launch (start us, length us, event | category | flops | bytes accessed | tf_op | source)
XLA Modules:
  0.0 183.0 jit_solution(18427909298086086471)
XLA Ops:
  0.6 0.7 convert_element_type.3
  1.3 0.7 pad_maximum_fusion
  2.0 0.7 copy.15.choices_ref
  2.7 176.5 %layer.1 = (bf16[128,2048]{1,0:T(8,128)(2,1)}, bf16[128,2048]{1,0:T(8,128)(2,1)}) custom-call(s32[16]{0:T(128)} %order_ref.1, bf16[128,2048]{1,0:T(8,128)(2,1)} %residual_ref.1, bf16[128,2048]{1,0:T(8,128)(2,1)} %queries_ref.1, bf16[128,256]{1,0:T(8,128)(2,1)} %keys_ref.1, bf16[128,256]{1,0:T(8,128)(2,1)} %values_ref.1, f32[128,16]{1,0:T(8,128)} %copy.15.choices_ref, ...), custom_call_target="tpu_custom_call" | custom-call | tf_op jit(solution)/shard_map/layer/pallas_call | solution.py:578
  179.2 1.9 %copy.18 = bf16[128,2048]{1,0:T(8,128)(2,1)} copy(bf16[128,2048]{1,0:T(8,128)(2,1)} %get-tuple-element.4) | data formatting | bytes 1048576
  181.1 1.9 %copy.19 = bf16[128,2048]{1,0:T(8,128)(2,1)} copy(bf16[128,2048]{1,0:T(8,128)(2,1)} %get-tuple-element.5) | data formatting | bytes 1048576

commit v6 on v5

--- a/solution.py
+++ b/solution.py
@@ -458,7 +458,8 @@
             p = plane_at(j, z, planes)
             second_forward(p).wait_recv()
             second_forward(p).start()
-            pl.when(j == planes - 1)(lambda: core_sum(z))
+            pl.when(j == planes - 2)(lambda: core_sum(z))
+            pl.when(j == planes - 1)(lambda: core_sum(plane_at(1, z, planes)))
             for row in range(2):
                 gather_copy(p * SEQS + row * 2 + 1 - c, c_s.at[0], at_core).wait_recv()
 
@@ -479,7 +480,7 @@
         core_sum(plane_at(planes - 1 - i, z, planes))
         return carry
 
-    lax.fori_loop(0, planes - 1, far_sum, 0)
+    lax.fori_loop(0, planes - 2, far_sum, 0)
 
     def chain(i, carry):
         p = plane_at(planes - 1 - i // HALVES, z, planes)
@@ -629,7 +630,9 @@
 
 def fits(devices, rows, width, hidden):
     blocks = 4 * devices + 8
-    return lax.axis_size("groups") == 2 and 2 * (blocks * rows * width + 3 * width * hidden) < VMEM_BYTES * 4 // 5
+    if lax.axis_size("groups") != 2 or devices < 3 * SEQS:
+        return False
+    return 2 * (blocks * rows * width + 3 * width * hidden) < VMEM_BYTES * 4 // 5
 
 
 def local(

time: 183 us -> 193 us (1.055)
  Pallas kernels: 176 us -> 186 us
    pallas_call x1, Pallas kernels: 176 us -> 186 us  [layer_call(): pl.pallas_call(functools.partial(layer_kernel, planes, cap), out_shape=[j...]
where the time goes in v6:
time: 193 us
  Pallas kernels  186 us (96%)
  local copies, waits for them, and re-layouts  4.49 us (2%)
    pallas_call x1, Pallas kernels, layer_call(): pl.pallas_call(functools.partial(layer_kernel, planes, cap), out_shape=[j...  186 us

profile of v6, /device:TPU:10, one launch (start us, length us, event | category | flops | bytes accessed | tf_op | source)
XLA Modules:
  0.0 192.5 jit_solution(14040805997914800483)
XLA Ops:
  0.6 0.7 convert_element_type.3
  1.3 0.7 pad_maximum_fusion
  2.0 0.7 copy.15.choices_ref
  2.7 186.0 %layer.1 = (bf16[128,2048]{1,0:T(8,128)(2,1)}, bf16[128,2048]{1,0:T(8,128)(2,1)}) custom-call(s32[16]{0:T(128)} %order_ref.1, bf16[128,2048]{1,0:T(8,128)(2,1)} %residual_ref.1, bf16[128,2048]{1,0:T(8,128)(2,1)} %queries_ref.1, bf16[128,256]{1,0:T(8,128)(2,1)} %keys_ref.1, bf16[128,256]{1,0:T(8,128)(2,1)} %values_ref.1, f32[128,16]{1,0:T(8,128)} %copy.15.choices_ref, ...), custom_call_target="tpu_custom_call" | custom-call | tf_op jit(solution)/shard_map/layer/pallas_call | solution.py:579
  188.8 1.9 copy.18
  190.7 1.9 copy.19
